TPU v7x, 32 devices: a whole 2x2x4 slice. The times are simulated.
32 devices in a mesh: grp: 2 (over x), own: 16 (over z, y, core).
Axes of the slice: x: 2, y: 2, z: 4, core: 2. Of those that a mesh axis runs over, the one named last changes fastest.
Arguments:
- coefficients: bfloat16 [64, 512, 4608], P('own', 'grp'), parts along dimension 1, may hold values from -6 to 6
- rotations: bfloat16 [64, 3342336], P('own'), may hold values from -0.75 to 0.75
- legendre: bfloat16 [256, 512, 512], P('own'), may hold values from -48 to 48, as said below
- degree_slot: int32 [8, 64], replicated, may hold values from 0 to 63, each once within a row
- column_order: int32 [512], P('grp'), parts along dimension 0, may hold values from 0 to 255, each once
Outputs:
- grid_errors: bfloat16 [512, 256, 1024], P('grp', 'own'), parts along dimension 0
There are 2 independent parts, one for each index of `grp`. A program takes and returns all parts, laid end to end along the dimension named above; an argument that names none is the same for every part. Nothing has to cross between parts.
Inputs may be any that keep to these rules, and one draw needn't show every extreme that they name: Each row is a permutation; slot s of class k holds degree 64 * k + degree_slot[k, s]. `column_order`: a permutation of the columns. legendre[t, m, l] is zero where l < m.
All inputs are finite; a program needn't handle non-finite values.
Results may differ from a plain program's by a relative error of at most 0.0062.
Values may be sent and summed in bfloat16 or wider, within the bound.
A program may use at most 192 MiB of HBM per device.

v0:
```python
import math

import jax
import jax.numpy as jnp
from jax import lax
from jax.sharding import PartitionSpec as P

BATCHES = 2


def rotate_bucket(chosen, rotations, degrees, bucket, slot_count):
    extent = 2 * slot_count * (bucket + 1)
    first_row = slot_count * bucket * (bucket + 1)
    offset = 4 * slot_count * slot_count * bucket * (bucket + 1) * (2 * bucket + 1) // 6
    block = chosen[:, :, first_row : first_row + extent]
    active = jnp.arange(extent, dtype=jnp.int32)[None, :] < (2 * degrees + 1)[:, None]
    block = jnp.where(active[:, None, :], block, jnp.zeros((), block.dtype))
    matrix = rotations[:, offset : offset + extent * extent].reshape(
        rotations.shape[0], extent, extent
    )
    turned = lax.dot_general(
        matrix, block, (((2,), (2,)), ((0,), (0,))), preferred_element_type=jnp.float32
    )
    return turned.astype(jnp.bfloat16)


def order_entries(turned, degrees, order_ids):
    extent = turned.shape[1]
    row_ids = jnp.arange(extent, dtype=jnp.int32)
    upward_valid = order_ids[None, :] <= degrees[:, None]
    downward_valid = upward_valid & (order_ids[None, :] >= 1)
    upward = (degrees[:, None] + order_ids[None, :])[:, :, None]
    downward = (degrees[:, None] - order_ids[None, :])[:, :, None]
    upward_pick = (row_ids[None, None, :] == upward) & upward_valid[:, :, None]
    downward_pick = (row_ids[None, None, :] == downward) & downward_valid[:, :, None]
    picker = jnp.stack([upward_pick, downward_pick], axis=2).astype(jnp.bfloat16)
    picked = jnp.einsum("smpj,sjc->smpc", picker, turned, preferred_element_type=jnp.float32)
    return picked.astype(jnp.bfloat16)


def local(coefficients, rotations, legendre, degree_slot, column_order):
    owners = lax.axis_size("own")
    own_index = lax.axis_index("own")
    slot_local = coefficients.shape[0]
    buckets = degree_slot.shape[0]
    slot_count = degree_slot.shape[1]
    orders = slot_count * buckets
    longitudes = 2 * orders
    order_local = orders // owners
    slot_ids = own_index * slot_local + jnp.arange(slot_local, dtype=jnp.int32)
    local_degrees = [
        slot_count * bucket + jnp.take(degree_slot[bucket], slot_ids) for bucket in range(buckets)
    ]
    positions = jnp.arange(orders, dtype=jnp.int32)
    degree_index = jnp.concatenate(
        [slot_count * bucket + degree_slot[bucket] for bucket in range(buckets)]
    )
    moved = lax.all_to_all(legendre, "own", split_axis=1, concat_axis=0, tiled=True)
    permuter = (positions[:, None] == degree_index[None, :]).astype(jnp.bfloat16)
    permuted = jnp.einsum(
        "til,ld->tid", moved, permuter, preferred_element_type=jnp.float32
    ).astype(jnp.bfloat16)
    legendre_rows = permuted.reshape(moved.shape[0], order_local, buckets, slot_count)

    def synthesize(received):
        summed = jnp.einsum(
            "tiks,skipc->tipc", legendre_rows, received, preferred_element_type=jnp.float32
        )
        return summed.astype(jnp.bfloat16)

    def regroup(chosen):
        pieces = []
        for bucket in range(buckets):
            turned = rotate_bucket(chosen, rotations, local_degrees[bucket], bucket, slot_count)
            pieces.append(order_entries(turned, local_degrees[bucket], positions))
        outgoing = jnp.stack(pieces, axis=1)
        return synthesize(lax.all_to_all(outgoing, "own", split_axis=2, concat_axis=0, tiled=True))

    longitude = jnp.arange(longitudes, dtype=jnp.int32)
    product_mod = positions[:, None] * longitude[None, :] % longitudes
    angles = product_mod.astype(jnp.float32) * (2.0 * math.pi / longitudes)
    fourier_table = (jnp.stack([jnp.cos(angles), jnp.sin(angles)], axis=1) / orders).astype(
        jnp.bfloat16
    )

    def transform(received):
        grid = jnp.einsum(
            "tmpc,mpn->ctn", received, fourier_table, preferred_element_type=jnp.float32
        )
        return grid.astype(jnp.bfloat16)

    def one_round(picked):
        chosen = jnp.take(coefficients, picked, axis=1)
        fourier = regroup(chosen)
        return transform(lax.all_to_all(fourier, "own", split_axis=0, concat_axis=1, tiled=True))

    batch_width = column_order.shape[0] // BATCHES
    outputs = [
        one_round(column_order[batch_index * batch_width : (batch_index + 1) * batch_width])
        for batch_index in range(BATCHES)
    ]
    return jnp.concatenate(outputs, axis=0)


def solution(mesh):
    placed = (P("own", "grp", None), P("own", None), P("own", None, None), P(), P("grp"))
    return jax.shard_map(
        local, mesh=mesh, in_specs=placed, out_specs=P("grp", "own", None), check_vma=False
    )
```

profile of v0, /device:TPU:13, one launch (start us, length us, event | category | flops | bytes accessed | tf_op | source)
XLA Modules:
  0.0 809.0 jit_solution(6779471936699436123)
XLA Ops:
  0.0 11.4 %copy.24 = bf16[16,512,512]{2,0,1:T(8,128)(2,1)} copy(bf16[16,512,512]{2,1,0:T(8,128)(2,1)} %param.11) | data formatting | bytes 16777216 | tf_op args[2]
  11.4 6.9 all-to-all-start.1
  28.8 6.9 slice.136
  35.7 6.9 slice.139
  42.5 8.1 slice.142
  60.9 13.7 %gather_fusion.9 = bf16[128,4,4608]{2,0,1:T(8,128)(2,1)} fusion(bf16[4,256,4608]{2,1,0:T(8,128)(2,1)} %param.9, s32[1024]{0:T(1024)S(1)} %get-tuple-element.84), kind=kCustom, calls=%fused_computation.9.clone | custom fusion | bytes 9437696 | tf_op jit(solution)/shard_map/jit(_take)/gather | solution.py:93
  124.4 5.3 fusion.121
  151.4 13.4 %fusion.127 = bf16[4,8,512,2,128]{4,2,3,0,1:T(8,128)(2,1)} fusion(bf16[4,8,512,2,128]{4,2,3,0,1:T(8,128)(2,1)} %fusion.99, bf16[1,4,1024,1024]{3,1,2,0:T(4,128)(2,1)} %bitcast.382, pred[4,512,1,1024]{3,1,2,0:T(32,128)(4,1)} %fusion.5, pred[4,512,1,1024]{3,1,2,0:T(32,128)(4,1)} %fusion.4, bf16[4,128,4608]{2,1,0:T(8,128)(2,1)} %select_bitcast_fusion, ...), kind=kOutput, calls=%fused_computation.157 | convolution fusion | flops 2153250816 | bytes 14684160 | tf_op jit(solution)/shard_map/smpj,sjc->smpc/dot_general | solution.py:37
  164.8 13.1 %copy.30 = bf16[4,8,512,2,128]{4,3,0,1,2:T(2,128)(2,1)} copy(bf16[4,8,512,2,128]{4,2,3,0,1:T(8,128)(2,1)} %fusion.127) | data formatting | bytes 16777216 | tf_op jit(solution)/shard_map/stack | solution.py:76
  177.9 22.6 %all-to-all-done.1 = bf16[16,512,512]{2,0,1:T(8,128)(2,1)} async-done(((bf16[16,512,512]{2,0,1:T(8,128)(2,1)}), bf16[16,512,512]{2,0,1:T(8,128)(2,1)}, u32[]{:S(2)}, u32[]{:S(2)}) %all-to-all-start.1) | async-done | bytes 8388640 | tf_op jit(solution)/shard_map/all_to_all | solution.py:58
  205.6 13.8 %gather_fusion.1 = bf16[128,4,4608]{2,0,1:T(8,128)(2,1)} fusion(bf16[4,256,4608]{2,1,0:T(8,128)(2,1)} %param.9, s32[1024]{0:T(1024)} %get-tuple-element.85), kind=kCustom, calls=%fused_computation.1.clone | custom fusion | bytes 9437696 | tf_op jit(solution)/shard_map/jit(_take)/gather | solution.py:93
  234.5 5.6 fusion.159
  240.1 5.3 fusion.139
  264.2 12.8 %fusion.133 = bf16[4,8,512,2,128]{4,2,3,0,1:T(8,128)(2,1)} fusion(bf16[4,8,512,2,128]{4,2,3,0,1:T(8,128)(2,1)} %fusion.101, bf16[1,4,1024,1024]{3,1,2,0:T(4,128)(2,1)} %bitcast.383, pred[4,512,1,1024]{3,1,2,0:T(32,128)(4,1)} %fusion.5, pred[4,512,1,1024]{3,1,2,0:T(32,128)(4,1)S(1)} %copy-done.2, bf16[4,128,4608]{2,1,0:T(8,128)(2,1)} %select_bitcast_fusion.1, ...), kind=kOutput, calls=%fused_computation.159 | convolution fusion | flops 2153250816 | bytes 14684160 | tf_op jit(solution)/shard_map/smpj,sjc->smpc/dot_general | solution.py:37
  277.0 13.2 %copy.22 = bf16[4,8,512,2,128]{4,3,0,1,2:T(2,128)(2,1)} copy(bf16[4,8,512,2,128]{4,2,3,0,1:T(8,128)(2,1)} %fusion.133) | data formatting | bytes 16777216 | tf_op jit(solution)/shard_map/stack | solution.py:76
  290.1 97.6 %all-to-all-done.3 = bf16[4,8,512,2,128]{4,3,0,1,2:T(2,128)(2,1)} async-done(((bf16[4,8,512,2,128]{4,3,0,1,2:T(2,128)(2,1)}), bf16[4,8,512,2,128]{4,3,0,1,2:T(2,128)(2,1)}, u32[]{:S(2)}, u32[]{:S(2)}) %all-to-all-start.3) | async-done | bytes 8388640 | tf_op jit(solution)/shard_map/all_to_all | solution.py:77
  393.1 8.1 copy.25
  401.2 9.6 %copy.31 = bf16[4,8,16,32,2,128]{5,0,2,1,4,3:T(4,128)(2,1)} copy(bf16[4,8,16,32,2,128]{5,4,0,1,3,2:T(2,128)(2,1)} %bitcast.79) | data formatting | bytes 16777216 | tf_op jit(solution)/shard_map/all_to_all | solution.py:77
  410.8 6.8 convolution_convert_fusion
  417.6 10.2 %fusion.30 = bf16[256,32,2,128]{0,3,2,1:T(8,128)(2,1)} fusion(bf16[64,8,32,2,128]{4,0,1,3,2:T(8,128)(2,1)} %bitcast.378, bf16[256,32,8,64,1]{0,3,2,4,1:T(8,128)(2,1)} %bitcast.376), kind=kOutput, calls=%fused_computation.62 | convolution fusion | flops 2149580800 | bytes 20971520 | tf_op jit(solution)/shard_map/tiks,skipc->tipc/dot_general | solution.py:66
  427.8 11.3 %copy.32 = bf16[256,32,2,128]{3,2,1,0:T(2,128)(2,1)} copy(bf16[256,32,2,128]{0,3,2,1:T(8,128)(2,1)} %fusion.30) | data formatting | bytes 8388608 | tf_op jit(solution)/shard_map/convert_element_type | solution.py:69
  439.1 136.1 %all-to-all-done = bf16[4,8,512,2,128]{4,3,0,1,2:T(2,128)(2,1)} async-done(((bf16[4,8,512,2,128]{4,3,0,1,2:T(2,128)(2,1)}), bf16[4,8,512,2,128]{4,3,0,1,2:T(2,128)(2,1)}, u32[]{:S(2)}, u32[]{:S(2)}) %all-to-all-start) | async-done | bytes 8388640 | tf_op jit(solution)/shard_map/all_to_all | solution.py:77
  580.1 8.3 %copy.23 = bf16[4,8,16,32,2,128]{5,0,2,1,4,3:T(4,128)(2,1)} copy(bf16[4,8,16,32,2,128]{5,4,0,1,3,2:T(2,128)(2,1)} %bitcast.34) | data formatting | bytes 16777216 | tf_op jit(solution)/shard_map/all_to_all | solution.py:77
  588.4 10.2 %fusion.28 = bf16[256,32,2,128]{0,3,2,1:T(8,128)(2,1)} fusion(bf16[64,8,32,2,128]{4,0,1,3,2:T(8,128)(2,1)} %bitcast.379, bf16[256,32,8,64,1]{0,3,2,4,1:T(8,128)(2,1)} %bitcast.377), kind=kOutput, calls=%fused_computation.60 | convolution fusion | flops 2149580800 | bytes 20971520 | tf_op jit(solution)/shard_map/tiks,skipc->tipc/dot_general | solution.py:66
  598.6 11.3 %copy.26 = bf16[256,32,2,128]{3,2,1,0:T(2,128)(2,1)} copy(bf16[256,32,2,128]{0,3,2,1:T(8,128)(2,1)} %fusion.28) | data formatting | bytes 8388608 | tf_op jit(solution)/shard_map/convert_element_type | solution.py:69
  609.9 62.6 %all-to-all-done.4 = bf16[256,32,2,128]{3,2,1,0:T(2,128)(2,1)} async-done(((bf16[256,32,2,128]{3,2,1,0:T(2,128)(2,1)}), bf16[256,32,2,128]{3,2,1,0:T(2,128)(2,1)}, u32[]{:S(2)}, u32[]{:S(2)}) %all-to-all-start.4) | async-done | bytes 4194336 | tf_op jit(solution)/shard_map/all_to_all | solution.py:95
  677.9 9.0 %fusion.188 = (f32[512,1,1024]{2,0,1:T(8,128)S(1)}, f32[512,1,1024]{2,0,1:T(8,128)}) fusion(), kind=kLoop, calls=%fused_computation.199 | loop fusion | flops 7340032 | bytes 4194304 | tf_op jit(solution)/shard_map/sin | solution.py:82
  693.2 77.0 %all-to-all-done.2 = bf16[256,32,2,128]{3,2,1,0:T(2,128)(2,1)} async-done(((bf16[256,32,2,128]{3,2,1,0:T(2,128)(2,1)}), bf16[256,32,2,128]{3,2,1,0:T(2,128)(2,1)}, u32[]{:S(2)}, u32[]{:S(2)}) %all-to-all-start.2) | async-done | bytes 4194336 | tf_op jit(solution)/shard_map/all_to_all | solution.py:95
  776.3 6.1 fusion.31
  782.4 6.5 fusion.29
  788.9 8.1 %pad_maximum_fusion = bf16[256,16,1024]{2,0,1:T(8,128)(2,1)} fusion(bf16[128,16,1024]{2,0,1:T(8,128)(2,1)} %fusion.31, bf16[128,16,1024]{2,0,1:T(8,128)(2,1)} %fusion.29), kind=kLoop, calls=%fused_computation.18 | loop fusion | flops 16777216 | bytes 16777216 | tf_op jit(solution)/shard_map/concatenate | solution.py:102
  797.0 11.5 %copy.36 = bf16[256,16,1024]{2,1,0:T(8,128)(2,1)} copy(bf16[256,16,1024]{2,0,1:T(8,128)(2,1)} %pad_maximum_fusion) | data formatting | bytes 16777216 | tf_op jit(solution)/shard_map/concatenate | solution.py:102
  (125 shorter events, 159.0 us)
Async XLA Ops:
  11.4 189.1 %all-to-all-start.1 = ((bf16[16,512,512]{2,0,1:T(8,128)(2,1)}), bf16[16,512,512]{2,0,1:T(8,128)(2,1)}, u32[]{:S(2)}, u32[]{:S(2)}) async-start(bf16[16,512,512]{2,0,1:T(8,128)(2,1)} %copy.24), calls=%async_computation.1 | async-start | bytes 16777216 | tf_op jit(solution)/shard_map/all_to_all | solution.py:58
  42.5 8.1 %copy-start.18 = (s32[256]{0:T(256)S(1)}, s32[256]{0:T(256)}, u32[]{:S(2)}) copy-start(s32[256]{0:T(256)} %param.13) | copy-start | bytes 3076
  42.5 8.7 %copy-start.8 = (s32[8,64]{1,0:T(8,128)S(1)}, s32[8,64]{1,0:T(8,128)}, u32[]{:S(2)}) copy-start(s32[8,64]{1,0:T(8,128)} %param.12) | copy-start | bytes 6148
  97.9 7.1 copy-start.17
  105.0 8.8 %copy-start.13 = (pred[4,768]{1,0:T(4,128)(4,1)S(1)}, pred[4,768]{1,0:T(4,128)(4,1)}, u32[]{:S(2)}) copy-start(pred[4,768]{1,0:T(4,128)(4,1)} %iota_compare_fusion.19) | copy-start | bytes 9220
  113.8 5.2 copy-start.16
  119.0 5.3 copy-start.14
  129.7 4.8 copy-start.10
  129.7 6.4 copy-start.9
  134.5 8.4 %copy-start.12 = (pred[4,896]{1,0:T(4,128)(4,1)S(1)}, pred[4,896]{1,0:T(4,128)(4,1)}, u32[]{:S(2)}) copy-start(pred[4,896]{1,0:T(4,128)(4,1)} %iota_compare_fusion.18) | copy-start | bytes 10756
  136.1 12.0 %copy-start.4 = (pred[4,512,1,896]{3,1,2,0:T(32,128)(4,1)}, pred[4,512,1,896]{3,1,2,0:T(32,128)(4,1)S(1)}, u32[]{:S(2)}) copy-start(pred[4,512,1,896]{3,1,2,0:T(32,128)(4,1)S(1)} %fusion.9) | copy-start | bytes 5505028
  137.7 10.4 %copy-start.6 = (pred[4,512,1,896]{3,1,2,0:T(32,128)(4,1)}, pred[4,512,1,896]{3,1,2,0:T(32,128)(4,1)S(1)}, u32[]{:S(2)}) copy-start(pred[4,512,1,896]{3,1,2,0:T(32,128)(4,1)S(1)} %fusion.8) | copy-start | bytes 5505028
  148.1 3.3 copy-start.11
  200.5 187.2 %all-to-all-start.3 = ((bf16[4,8,512,2,128]{4,3,0,1,2:T(2,128)(2,1)}), bf16[4,8,512,2,128]{4,3,0,1,2:T(2,128)(2,1)}, u32[]{:S(2)}, u32[]{:S(2)}) async-start(bf16[4,8,512,2,128]{4,3,0,1,2:T(2,128)(2,1)} %copy.30), calls=%async_computation.3 | async-start | bytes 16777216 | tf_op jit(solution)/shard_map/all_to_all | solution.py:77
  205.6 13.8 %copy-start.15 = (pred[128]{0:T(512)(128)(4,1)S(1)}, pred[128]{0:T(512)(128)(4,1)}, u32[]{:S(2)}) copy-start(pred[128]{0:T(512)(128)(4,1)} %get-tuple-element.6) | copy-start | bytes 388
  219.4 5.0 copy-start.20
  219.4 7.6 copy-start.19
  255.6 5.3 copy-start.5
  255.6 5.3 copy-start.7
  260.9 3.3 copy-start.2
  387.7 187.5 %all-to-all-start = ((bf16[4,8,512,2,128]{4,3,0,1,2:T(2,128)(2,1)}), bf16[4,8,512,2,128]{4,3,0,1,2:T(2,128)(2,1)}, u32[]{:S(2)}, u32[]{:S(2)}) async-start(bf16[4,8,512,2,128]{4,3,0,1,2:T(2,128)(2,1)} %copy.22), calls=%async_computation | async-start | bytes 16777216 | tf_op jit(solution)/shard_map/all_to_all | solution.py:77
  401.2 9.6 %copy-start = (bf16[16,16,32,512]{3,0,1,2:T(8,128)(2,1)S(1)}, bf16[16,16,32,512]{3,0,1,2:T(8,128)(2,1)}, u32[]{:S(2)}) copy-start(bf16[16,16,32,512]{3,0,1,2:T(8,128)(2,1)} %copy.25) | copy-start | bytes 25165828
  575.2 97.4 %all-to-all-start.4 = ((bf16[256,32,2,128]{3,2,1,0:T(2,128)(2,1)}), bf16[256,32,2,128]{3,2,1,0:T(2,128)(2,1)}, u32[]{:S(2)}, u32[]{:S(2)}) async-start(bf16[256,32,2,128]{3,2,1,0:T(2,128)(2,1)} %copy.32), calls=%async_computation.4 | async-start | bytes 8388608 | tf_op jit(solution)/shard_map/all_to_all | solution.py:95
  672.6 97.6 %all-to-all-start.2 = ((bf16[256,32,2,128]{3,2,1,0:T(2,128)(2,1)}), bf16[256,32,2,128]{3,2,1,0:T(2,128)(2,1)}, u32[]{:S(2)}, u32[]{:S(2)}) async-start(bf16[256,32,2,128]{3,2,1,0:T(2,128)(2,1)} %copy.26), calls=%async_computation.2 | async-start | bytes 8388608 | tf_op jit(solution)/shard_map/all_to_all | solution.py:95
  773.4 2.2 copy-start.1
  773.4 2.9 copy-start.3
where the time goes:
time: 815 us; the launch traced here: 809 us
  waiting for transfers between devices  396 us (49%)
  local copies, waits for them, and re-layouts  176 us (22%)
  matrix products  145 us (18%)
  other arithmetic  63.6 us (8%)
  starting transfers between devices  27.4 us (3%)
    all_to_all x2, waiting for transfers between devices, regroup(): lax.all_to_all(outgoing, 'own', split_axis=2, concat_axis=0, tiled=True)  234 us
    all_to_all x2, waiting for transfers between devices, one_round(): lax.all_to_all(fourier, 'own', split_axis=0, concat_axis=1, tiled=True)  140 us
    dot_general x16, matrix products, order_entries(): jnp.einsum('smpj,sjc->smpc', picker, turned, preferred_element_type=jnp.f...  84 us
    slice x7, local copies, waits for them, and re-layouts, rotate_bucket(): rotations[:, offset:offset + extent * extent]  32.3 us
    gather x2, local copies, waits for them, and re-layouts, one_round(): chosen = jnp.take(coefficients, picked, axis=1)  27.4 us
    another operation x2, local copies, waits for them, and re-layouts, regroup(): outgoing = jnp.stack(pieces, axis=1)  26.3 us
    all_to_all x1, waiting for transfers between devices, local(): lax.all_to_all(legendre, 'own', split_axis=1, concat_axis=0, tiled=True)  22.6 us
    convert_element_type x2, local copies, waits for them, and re-layouts, synthesize(): return summed.astype(jnp.bfloat16)  22.6 us
  transfers between devices with their start and end apart: 5, of which 5 were waited for; matrix products, arithmetic and copies ran while one was open for 41% of the time, Pallas kernels for 0%

commit v1 on v0

v1 whole, which is shorter than its diff:
```python
import math

import jax
import jax.numpy as jnp
import numpy as np
from jax import lax
from jax.experimental import pallas as pl
from jax.experimental.pallas import tpu as pltpu
from jax.sharding import PartitionSpec as P

VMEM_BYTES = 56 * 1024 * 1024


def class_extent(bucket, slot_count):
    return 2 * slot_count * (bucket + 1)


def class_first(bucket, slot_count):
    return slot_count * bucket * (bucket + 1)


def class_offset(bucket, slot_count):
    return 4 * slot_count * slot_count * bucket * (bucket + 1) * (2 * bucket + 1) // 6


def signed_orders(bucket, slot_count, owners):
    share = slot_count // owners
    owner, block, inner, part = np.meshgrid(
        np.arange(owners), np.arange(bucket + 1), np.arange(share), np.arange(2), indexing="ij"
    )
    order = slot_count * block + share * owner + inner
    signed = np.where(part == 0, order, -order)
    signed = np.where((part == 1) & (order == 0), 1 << 20, signed)
    return signed.reshape(-1, 1).astype(np.int32)


def rotate_classes(coefficients, rotations, degrees, column_pick, classes, slot_count, owners):
    slot_local, columns, slot_rows = coefficients.shape
    extents = [class_extent(k, slot_count) for k in classes]
    count = len(classes)

    def kernel(degree_ref, coef_ref, pick_ref, *refs):
        matrices, orders, outs = refs[:count], refs[count : 2 * count], refs[2 * count :]
        slot = pl.program_id(0)
        for index, bucket in enumerate(classes):
            extent = extents[index]
            degree = degree_ref[bucket, slot]
            first = class_first(bucket, slot_count)
            block = coef_ref[0, :, first : first + extent]
            lanes = lax.broadcasted_iota(jnp.int32, block.shape, 1)
            block = jnp.where(lanes <= 2 * degree, block, jnp.zeros((), block.dtype))
            turned = lax.dot_general(
                matrices[index][0], block, (((1,), (1,)), ((), ())), preferred_element_type=jnp.float32
            ).astype(jnp.bfloat16)
            turned = jnp.dot(turned, pick_ref[...], preferred_element_type=jnp.float32).astype(jnp.bfloat16)
            target = degree + orders[index][...]
            target = jnp.where(target <= 2 * degree, target, -1)
            rows = lax.broadcasted_iota(jnp.int32, (extent, extent), 1)
            picker = (rows == target).astype(jnp.float32).astype(jnp.bfloat16)
            outs[index][0] = jnp.dot(picker, turned, preferred_element_type=jnp.float32).astype(jnp.bfloat16)

    matrices, orders = [], []
    for bucket, extent in zip(classes, extents):
        offset = class_offset(bucket, slot_count)
        matrices.append(
            rotations[:, offset : offset + extent * extent].reshape(slot_local, extent, extent)
        )
        orders.append(jnp.asarray(signed_orders(bucket, slot_count, owners)))
    by_slot = lambda s, _: (s, 0, 0)
    fixed = lambda s, _: (0, 0)
    return pl.pallas_call(
        kernel,
        grid_spec=pltpu.PrefetchScalarGridSpec(
            num_scalar_prefetch=1,
            grid=(slot_local,),
            in_specs=[
                pl.BlockSpec((1, columns, slot_rows), by_slot),
                pl.BlockSpec((columns, columns), fixed),
                *[pl.BlockSpec((1, n, n), by_slot) for n in extents],
                *[pl.BlockSpec((n, 1), fixed) for n in extents],
            ],
            out_specs=[pl.BlockSpec((1, n, columns), by_slot) for n in extents],
        ),
        out_shape=[jax.ShapeDtypeStruct((slot_local, n, columns), jnp.bfloat16) for n in extents],
        compiler_params=pltpu.CompilerParams(vmem_limit_bytes=VMEM_BYTES),
        cost_estimate=pl.CostEstimate(
            flops=4 * slot_local * columns * sum(n * n for n in extents),
            bytes_accessed=2 * slot_local * sum(n * n + 2 * n * columns for n in extents),
            transcendentals=0,
        ),
    )(degrees, coefficients, column_pick, *matrices, *orders)


def transform(parts, tables):
    owners, latitudes, _, columns = parts[0].shape
    longitudes = tables[0].shape[1]
    if any(part.shape[2] % 16 for part in parts):
        grid = sum(
            jnp.einsum(
                "otrc,orn->ctn",
                part,
                table.reshape(owners, part.shape[2], longitudes),
                preferred_element_type=jnp.float32,
            )
            for part, table in zip(parts, tables)
        )
        return grid.astype(jnp.bfloat16)
    count = len(parts)
    width = 128
    tiles = longitudes // 128

    def kernel(*refs):
        part_refs, table_refs, out_ref, total = refs[:count], refs[count : 2 * count], refs[-2], refs[-1]
        for t in range(latitudes):
            value = None
            for part_ref, table_ref in zip(part_refs, table_refs):
                rows = part_ref[:, t].reshape(table_ref.shape[0], width)
                term = lax.dot_general(
                    rows, table_ref[...], (((0,), (0,)), ((), ())), preferred_element_type=jnp.float32
                )
                value = term if value is None else value + term
            for tile in range(tiles):
                total[pl.ds(tile * width * latitudes + t, width, stride=latitudes), :] = value[
                    :, tile * 128 : (tile + 1) * 128
                ]
        for tile in range(tiles):
            out_ref[:, :, tile * 128 : (tile + 1) * 128] = (
                total[tile * width * latitudes : (tile + 1) * width * latitudes, :]
                .reshape(width, latitudes, 128)
                .astype(jnp.bfloat16)
            )

    return pl.pallas_call(
        kernel,
        grid=(columns // width,),
        in_specs=[
            *[pl.BlockSpec((owners, latitudes, part.shape[2], width), lambda c: (0, 0, 0, c)) for part in parts],
            *[pl.BlockSpec(table.shape, lambda c: (0, 0)) for table in tables],
        ],
        out_specs=pl.BlockSpec((width, latitudes, longitudes), lambda c: (c, 0, 0)),
        out_shape=jax.ShapeDtypeStruct((columns, latitudes, longitudes), jnp.bfloat16),
        scratch_shapes=[pltpu.VMEM((tiles * width * latitudes, 128), jnp.float32)],
        compiler_params=pltpu.CompilerParams(vmem_limit_bytes=VMEM_BYTES),
    )(*parts, *tables)


def local(coefficients, rotations, legendre, degree_slot, column_order):
    owners = lax.axis_size("own")
    groups = lax.axis_size("grp")
    own_index = lax.axis_index("own")
    slot_local, columns, _ = coefficients.shape
    buckets, slot_count = degree_slot.shape
    orders = slot_count * buckets
    longitudes = 2 * orders
    latitudes = legendre.shape[0]
    share = slot_count // owners

    shared = latitudes % groups == 0
    mine = legendre
    if shared:
        mine = lax.dynamic_slice_in_dim(
            legendre, lax.axis_index("grp") * (latitudes // groups), latitudes // groups, axis=0
        )
    mine = mine.reshape(mine.shape[0], buckets, owners, share, orders)
    packed = jnp.concatenate([mine[:, b, :, :, slot_count * b :] for b in range(buckets)], axis=-1)
    lanes = packed.shape[-1]
    packed = packed.transpose(1, 0, 2, 3).reshape(owners, -1, lanes)
    moved = lax.all_to_all(packed, "own", split_axis=0, concat_axis=0, tiled=True)

    degrees = lax.dynamic_slice_in_dim(degree_slot, own_index * slot_local, slot_local, axis=1)
    degrees = degrees + slot_count * jnp.arange(buckets, dtype=jnp.int32)[:, None]
    column_ids = jnp.arange(columns, dtype=jnp.int32)
    column_pick = (column_ids[:, None] == column_order[None, :]).astype(jnp.bfloat16)

    high = buckets - buckets // 4
    chunks = [list(range(buckets - 1, high - 1, -1)), list(range(high - 1, -1, -1))]
    received = {}
    for classes in chunks:
        rotated = rotate_classes(
            coefficients, rotations, degrees, column_pick, classes, slot_count, owners
        )
        outgoing = jnp.concatenate(
            [part.reshape(slot_local, owners, -1, columns) for part in rotated], axis=2
        ).transpose(1, 0, 2, 3)
        arrived = lax.all_to_all(outgoing, "own", split_axis=0, concat_axis=0, tiled=True)
        arrived = arrived.reshape(owners * slot_local, -1, columns)
        start = 0
        for bucket in classes:
            size = (bucket + 1) * share * 2
            received[bucket] = arrived[:, start : start + size].reshape(
                owners * slot_local, bucket + 1, share, 2, columns
            )
            start += size

    if shared:
        moved = lax.all_gather(moved, "grp", axis=0, tiled=False)
        moved = moved.reshape(groups, owners, latitudes // groups, share, lanes)
        moved = moved.transpose(1, 0, 2, 3, 4)
    moved = moved.reshape(owners * latitudes, share, lanes)
    degree_ids = jnp.arange(slot_count, dtype=jnp.int32)
    permuters = (degree_ids[None, :, None] == degree_slot[:, None, :]).astype(jnp.bfloat16)

    def synthesize(blocks):
        pieces = []
        for block in blocks:
            start = slot_count * (block * buckets - block * (block - 1) // 2)
            count = buckets - block
            rows = moved[:, :, start : start + slot_count * count]
            rows = rows.reshape(owners * latitudes, share, count, slot_count)
            rows = jnp.einsum(
                "tikl,kls->tiks", rows, permuters[block:], preferred_element_type=jnp.float32
            ).astype(jnp.bfloat16)
            values = jnp.stack([received[k][:, block] for k in range(block, buckets)], axis=0)
            summed = jnp.einsum("tiks,ksipc->tipc", rows, values, preferred_element_type=jnp.float32)
            pieces.append(summed.astype(jnp.bfloat16).reshape(owners, latitudes, share * 2, columns))
        outgoing = jnp.concatenate(pieces, axis=2)
        return lax.all_to_all(outgoing, "own", split_axis=0, concat_axis=0, tiled=True)

    longitude = jnp.arange(longitudes, dtype=jnp.int32)
    low = buckets // 4
    groups_of_blocks = [
        list(range(high, buckets)),
        list(range(low, high)),
        list(range(low)),
    ]
    parts, tables = [], []
    for blocks in groups_of_blocks:
        parts.append(synthesize(blocks))
        held = (
            slot_count * jnp.asarray(blocks, jnp.int32)[None, :, None]
            + share * jnp.arange(owners, dtype=jnp.int32)[:, None, None]
            + jnp.arange(share, dtype=jnp.int32)[None, None, :]
        ).reshape(-1)
        product_mod = held[:, None] * longitude[None, :] % longitudes
        angles = product_mod.astype(jnp.float32) * (2.0 * math.pi / longitudes)
        table = jnp.stack([jnp.cos(angles), jnp.sin(angles)], axis=1) / orders
        tables.append(table.astype(jnp.bfloat16).reshape(-1, longitudes))
    return transform(parts, tables)


def solution(mesh):
    placed = (P("own", "grp", None), P("own", None), P("own", None, None), P(), P("grp"))
    return jax.shard_map(
        local, mesh=mesh, in_specs=placed, out_specs=P("grp", "own", None), check_vma=False
    )
```

time: 815 us -> 543 us (0.67)
  waiting for transfers between devices: 396 us -> 243 us
  matrix products: 145 us -> 20.5 us
  Pallas kernels: 0 us -> 60.7 us
  other arithmetic: 63.6 us -> 22.3 us
  local copies, waits for them, and re-layouts: 176 us -> 141 us
  between operations: 0.82 us -> 14.4 us
    all_to_all x5 -> x6, waiting for transfers between devices: 396 us -> 186 us  [the longest x3 92.8 us: synthesize(): lax.all_to_all(outgoing, 'own', split_axis=0, concat_axis=0, tiled=True)]
    dot_general x25 -> x14, matrix products: 145 us -> 20.5 us  [the longest x8 11.7 us: synthesize(): jnp.einsum('tiks,ksipc->tipc', rows, values, preferred_element_type=jnp.f...]
    pallas_call x0 -> x3, Pallas kernels: none -> 60.7 us  [the longest x2 36.8 us: rotate_classes(): pl.pallas_call(kernel, grid_spec=pltpu.PrefetchScalarGridSpec(num_scalar_...]
    all_gather x0 -> x1, waiting for transfers between devices: none -> 57.1 us  [local(): moved = lax.all_gather(moved, 'grp', axis=0, tiled=False)]
    gather x10 -> x0, local copies, waits for them, and re-layouts: 32.5 us -> none  [the longest x2 27.4 us: one_round(): chosen = jnp.take(coefficients, picked, axis=1)]
    all_to_all x7 -> x1, local copies, waits for them, and re-layouts: 36.5 us -> 4.37 us  [local(): lax.all_to_all(packed, 'own', split_axis=0, concat_axis=0, tiled=True)]
    and x17 -> x0, other arithmetic: 29.3 us -> none  [the longest x8 14.7 us: order_entries(): upward_pick = (row_ids[None, None, :] == upward) & upward_valid[:, :, None]]
    unnamed x44 -> x74, local copies, waits for them, and re-layouts: 14.3 us -> 40.4 us
  transfers between devices with their start and end apart: 5 -> 7, of which waited for: 5 -> 7; matrix products, arithmetic and copies ran while one was open for 41% -> 29% of each run, Pallas kernels for 0% -> 7%
where the time goes in v1:
time: 543 us; the launch traced here: 536 us
  waiting for transfers between devices  243 us (45%)
  local copies, waits for them, and re-layouts  141 us (26%)
  Pallas kernels  60.7 us (11%)
  starting transfers between devices  33.4 us (6%)
  other arithmetic  22.3 us (4%)
  matrix products  20.5 us (4%)
  between operations  14.4 us (3%)
    all_to_all x3, waiting for transfers between devices, synthesize(): lax.all_to_all(outgoing, 'own', split_axis=0, concat_axis=0, tiled=True)  92.8 us
    all_to_all x2, waiting for transfers between devices, local(): lax.all_to_all(outgoing, 'own', split_axis=0, concat_axis=0, tiled=True)  87 us
    all_gather x1, waiting for transfers between devices, local(): moved = lax.all_gather(moved, 'grp', axis=0, tiled=False)  57.1 us
    unnamed x74, local copies, waits for them, and re-layouts  40.4 us
    pallas_call x2, Pallas kernels, rotate_classes(): pl.pallas_call(kernel, grid_spec=pltpu.PrefetchScalarGridSpec(num_scalar_...  36.8 us
    pallas_call x1, Pallas kernels, transform(): pl.pallas_call(kernel, grid=(columns // width,), in_specs=[*[pl.BlockSpec...  23.9 us
    slice x14, local copies, waits for them, and re-layouts, synthesize(): rows = moved[:, :, start:start + slot_count * count]  20.9 us
    all_to_all x3, starting transfers between devices, synthesize(): lax.all_to_all(outgoing, 'own', split_axis=0, concat_axis=0, tiled=True)  15.8 us
  transfers between devices with their start and end apart: 7, of which 7 were waited for; matrix products, arithmetic and copies ran while one was open for 29% of the time, Pallas kernels for 7%

profile of v1, /device:TPU:13, one launch (start us, length us, event | category | flops | bytes accessed | tf_op | source)
XLA Modules:
  0.0 535.9 jit_solution(11236661827633059565)
XLA Ops:
  6.5 2.6 constant_dynamic-slice_fusion
  16.1 3.7 concatenate.19
  23.2 7.2 %all-to-all-start.1 = ((bf16[16,32,2304]{2,1,0:T(8,128)(2,1)}), bf16[16,32,2304]{2,1,0:T(8,128)(2,1)}, u32[]{:S(2)}, u32[]{:S(2)}) async-start(bf16[16,32,2304]{2,1,0:T(8,128)(2,1)} %copy.164), calls=%async_computation.1 | async-start | bytes 4718592 | tf_op jit(solution)/shard_map/all_to_all | solution.py:168
  30.4 8.1 %slice.222 = bf16[4,1048576]{1,0:T(4,128)(2,1)} slice(bf16[4,3342336]{1,0:T(4,128)(2,1)} %param.17), slice={[0:4], [2293760:3342336]} | slice | bytes 16777216 | tf_op jit(solution)/shard_map/slice | solution.py:66
  38.5 9.7 %copy.297 = bf16[1,4,1024,1024]{3,2,1,0:T(8,128)(2,1)} copy(bf16[1,4,1024,1024]{3,1,2,0:T(4,128)(2,1)} %bitcast.349) | data formatting | bytes 16777216
  48.2 3.6 copy.298
  53.1 20.2 %shard_map.154 = (bf16[4,1024,256]{2,1,0:T(8,128)(2,1)}, bf16[4,896,256]{2,1,0:T(8,128)(2,1)}) custom-call(s32[8,4]{1,0:T(8,128)} %dynamic-slice_add_fusion.degree_ref, bf16[4,256,4608]{2,1,0:T(8,128)(2,1)} %coef_ref.3, bf16[256,256]{1,0:T(8,128)(2,1)} %fusion.95.pick_ref, bf16[4,1024,1024]{2,1,0:T(8,128)(2,1)} %bitcast.378, bf16[4,896,896]{2,1,0:T(8,128)(2,1)} %bitcast.384, ...), custom_call_target="tpu_custom_call" | custom-call | flops 7583301632 | bytes 22675456 | tf_op jit(solution)/shard_map/pallas_call | solution.py:71
  73.3 3.6 copy_bitcast_fusion.4
  76.9 6.6 %all-to-all-done.1 = bf16[16,32,2304]{2,1,0:T(8,128)(2,1)} async-done(((bf16[16,32,2304]{2,1,0:T(8,128)(2,1)}), bf16[16,32,2304]{2,1,0:T(8,128)(2,1)}, u32[]{:S(2)}, u32[]{:S(2)}) %all-to-all-start.1) | async-done | bytes 2359328 | tf_op jit(solution)/shard_map/all_to_all | solution.py:168
  83.4 5.2 all-to-all-start
  91.0 2.8 copy.300
  101.4 16.7 %shard_map.155 = (bf16[4,768,256]{2,1,0:T(8,128)(2,1)}, bf16[4,640,256]{2,1,0:T(8,128)(2,1)}, bf16[4,512,256]{2,1,0:T(8,128)(2,1)}, bf16[4,384,256]{2,1,0:T(8,12...) custom-call(s32[8,4]{1,0:T(8,128)} %dynamic-slice_add_fusion.degree_ref, ...), custom_call_target="tpu_custom_call" | custom-call | flops 6106906624 | bytes 22937600 | tf_op jit(solution)/shard_map/pallas_call | solution.py:71
  122.0 3.0 copy.299
  125.0 50.3 %all-to-all-done = bf16[16,4,120,256]{3,2,1,0:T(8,128)(2,1)} async-done(((bf16[16,4,120,256]{3,2,1,0:T(8,128)(2,1)}), bf16[16,4,120,256]{3,2,1,0:T(8,128)(2,1)}, u32[]{:S(2)}, u32[]{:S(2)}) %all-to-all-start) | async-done | bytes 3932192 | tf_op jit(solution)/shard_map/all_to_all | solution.py:185
  175.3 4.9 all-to-all-start.3
  180.5 4.4 copy.165
  191.2 57.1 %all-gather.3.cloned.1.call-done = bf16[32,32,2304]{2,0,1:T(8,128)(2,1)} async-done(((bf16[16,32,2304]{2,0,1:T(8,128)(2,1)}), bf16[32,32,2304]{2,0,1:T(8,128)(2,1)}) %all-gather.3.cloned.1.call-update) | async-done | bytes 4718608 | tf_op jit(solution)/shard_map/all_gather | solution.py:196
  248.3 4.9 copy.166
  264.1 36.7 %all-to-all-done.3 = bf16[16,4,168,256]{3,2,1,0:T(8,128)(2,1)} async-done(((bf16[16,4,168,256]{3,2,1,0:T(8,128)(2,1)}), bf16[16,4,168,256]{3,2,1,0:T(8,128)(2,1)}, u32[]{:S(2)}, u32[]{:S(2)}) %all-to-all-start.3) | async-done | bytes 5505056 | tf_op jit(solution)/shard_map/all_to_all | solution.py:185
  300.8 5.2 all-to-all-start.2
  314.3 2.5 fusion.2
  338.3 2.5 fusion.33
  345.2 3.1 pad_maximum_fusion.3
  348.3 5.1 all-to-all-done.2.refs_0_
  354.7 5.5 %all-to-all-start.5 = ((bf16[16,16,16,256]{3,2,1,0:T(8,128)(2,1)}), bf16[16,16,16,256]{3,2,1,0:T(8,128)(2,1)}, u32[]{:S(2)}, u32[]{:S(2)}) async-start(bf16[16,16,16,256]{3,2,1,0:T(8,128)(2,1)} %pad_maximum_fusion.3), calls=%async_computation.5 | async-start | bytes 4194304 | tf_op jit(solution)/shard_map/all_to_all | solution.py:217
  361.7 2.4 slice.331
  393.5 3.5 pad_maximum_fusion
  396.9 10.6 %all-to-all-done.5.refs_2_ = bf16[16,16,16,256]{3,2,1,0:T(8,128)(2,1)} async-done(((bf16[16,16,16,256]{3,2,1,0:T(8,128)(2,1)}), bf16[16,16,16,256]{3,2,1,0:T(8,128)(2,1)}, u32[]{:S(2)}, u32[]{:S(2)}) %all-to-all-start.5) | async-done | bytes 2097184 | tf_op jit(solution)/shard_map/all_to_all | solution.py:217
  407.6 5.1 all-to-all-start.4
  420.9 4.2 fusion.58
  427.9 77.1 %all-to-all-done.4.refs_1_ = bf16[16,16,32,256]{3,2,1,0:T(8,128)(2,1)} async-done(((bf16[16,16,32,256]{3,2,1,0:T(8,128)(2,1)}), bf16[16,16,32,256]{3,2,1,0:T(8,128)(2,1)}, u32[]{:S(2)}, u32[]{:S(2)}) %all-to-all-start.4) | async-done | bytes 4194336 | tf_op jit(solution)/shard_map/all_to_all | solution.py:217
  504.9 23.9 %shard_map.156 = bf16[256,16,1024]{2,1,0:T(8,128)(2,1)} custom-call(bf16[16,16,16,256]{3,2,1,0:T(8,128)(2,1)} %copy-done.1, bf16[16,16,32,256]{3,2,1,0:T(8,128)(2,1)} %all-to-all-done.4.refs_1_, bf16[16,16,16,256]{3,2,1,0:T(8,128)(2,1)} %all-to-all-done.5.refs_2_, bf16[256,1024]{1,0:T(8,128)(2,1)} %convert_element_type.202.refs_3_, ...), custom_call_target="tpu_custom_call" | custom-call | tf_op jit(solution)/shard_map/pallas_call | solution.py:133
  (185 shorter events, 119.7 us)
Async XLA Ops:
  23.2 60.2 %all-to-all-start.1 = ((bf16[16,32,2304]{2,1,0:T(8,128)(2,1)}), bf16[16,32,2304]{2,1,0:T(8,128)(2,1)}, u32[]{:S(2)}, u32[]{:S(2)}) async-start(bf16[16,32,2304]{2,1,0:T(8,128)(2,1)} %copy.164), calls=%async_computation.1 | async-start | bytes 4718592 | tf_op jit(solution)/shard_map/all_to_all | solution.py:168
  38.5 9.7 %slice-start = ((bf16[4,3342336]{1,0:T(4,128)(2,1)}), bf16[4,802816]{1,0:T(4,128)(2,1)S(1)}, s32[]{:S(2)}) async-start(bf16[4,3342336]{1,0:T(4,128)(2,1)} %param.17), calls=%async_computation.7 | async-start | bytes 12845056 | tf_op jit(solution)/shard_map/slice | solution.py:66
  48.2 3.6 copy-start.22
  48.2 4.2 copy-start.23
  83.4 91.9 %all-to-all-start = ((bf16[16,4,120,256]{3,2,1,0:T(8,128)(2,1)}), bf16[16,4,120,256]{3,2,1,0:T(8,128)(2,1)}, u32[]{:S(2)}, u32[]{:S(2)}) async-start(bf16[16,4,120,256]{3,2,1,0:T(8,128)(2,1)} %copy_bitcast_fusion.4), calls=%async_computation | async-start | bytes 7864320 | tf_op jit(solution)/shard_map/all_to_all | solution.py:185
  88.6 2.3 slice-start.1
  91.0 2.9 slice-start.2
  93.8 2.1 slice-start.3
  95.9 1.8 slice-start.4
  118.1 1.8 copy-start.12
  119.7 1.3 copy-start.13
  119.9 1.3 copy-start.14
  120.0 1.4 copy-start.15
  175.3 125.4 %all-to-all-start.3 = ((bf16[16,4,168,256]{3,2,1,0:T(8,128)(2,1)}), bf16[16,4,168,256]{3,2,1,0:T(8,128)(2,1)}, u32[]{:S(2)}, u32[]{:S(2)}) async-start(bf16[16,4,168,256]{3,2,1,0:T(8,128)(2,1)} %bitcast.356), calls=%async_computation.3 | async-start | bytes 11010048 | tf_op jit(solution)/shard_map/all_to_all | solution.py:185
  180.2 68.0 %all-gather.3.cloned.1.call-start = ((), (), s32[]{:S(2)}) async-start(), calls=%async_computation.6 | async-start | bytes 7077888 | tf_op jit(solution)/shard_map/all_gather | solution.py:196
  190.0 69.6 %copy-start.2 = (bf16[64,64,256]{2,0,1:T(8,128)(2,1)}, bf16[64,64,256]{2,0,1:T(8,128)(2,1)S(1)}, u32[]{:S(2)}) copy-start(bf16[64,64,256]{2,0,1:T(8,128)(2,1)S(1)} %copy.160) | copy-start | bytes 6291460
  253.2 2.2 copy-start
  300.8 52.6 %all-to-all-start.2 = ((bf16[16,16,16,256]{3,2,1,0:T(8,128)(2,1)}), bf16[16,16,16,256]{3,2,1,0:T(8,128)(2,1)S(1)}, u32[]{:S(2)}, u32[]{:S(2)}) async-start(bf16[16,16,16,256]{3,2,1,0:T(8,128)(2,1)} %pad_maximum_fusion.2), calls=%async_computation.2 | async-start | bytes 4194304 | tf_op jit(solution)/shard_map/all_to_all | solution.py:217
  327.0 1.8 copy-start.5
  327.8 1.7 copy-start.3
  331.9 1.2 copy-start.21
  353.4 1.3 copy-start.1
  354.7 52.9 %all-to-all-start.5 = ((bf16[16,16,16,256]{3,2,1,0:T(8,128)(2,1)}), bf16[16,16,16,256]{3,2,1,0:T(8,128)(2,1)}, u32[]{:S(2)}, u32[]{:S(2)}) async-start(bf16[16,16,16,256]{3,2,1,0:T(8,128)(2,1)} %pad_maximum_fusion.3), calls=%async_computation.5 | async-start | bytes 4194304 | tf_op jit(solution)/shard_map/all_to_all | solution.py:217
  373.8 3.8 copy-start.10
  388.2 2.3 copy-start.16
  388.2 2.3 copy-start.17
  388.2 2.3 copy-start.18
  388.2 2.3 copy-start.20
  391.1 2.3 copy-start.8
  396.9 15.7 %copy-start.25 = (s32[2]{0:T(128)S(1)}, s32[2]{0:T(128)}, u32[]{:S(2)}) copy-start(s32[2]{0:T(128)} %constant.93) | copy-start | bytes 28
  407.6 97.4 %all-to-all-start.4 = ((bf16[16,16,32,256]{3,2,1,0:T(8,128)(2,1)}), bf16[16,16,32,256]{3,2,1,0:T(8,128)(2,1)}, u32[]{:S(2)}, u32[]{:S(2)}) async-start(bf16[16,16,32,256]{3,2,1,0:T(8,128)(2,1)} %pad_maximum_fusion), calls=%async_computation.4 | async-start | bytes 8388608 | tf_op jit(solution)/shard_map/all_to_all | solution.py:217
  418.9 1.7 copy-start.24
  (7 other events, 8.1 us)
Sparse Core Ops, SparseCore 0:
  185.0 63.2 all-gather.2

commit v2 on v1

--- a/solution.py
+++ b/solution.py
@@ -105,43 +105,67 @@
             for part, table in zip(parts, tables)
         )
         return grid.astype(jnp.bfloat16)
-    count = len(parts)
-    width = 128
-    tiles = longitudes // 128
-
-    def kernel(*refs):
-        part_refs, table_refs, out_ref, total = refs[:count], refs[count : 2 * count], refs[-2], refs[-1]
+    width = 256
+
+    def term(part_ref, table_ref, t):
+        rows = part_ref[:, t].reshape(table_ref.shape[0], columns)
+        return lax.dot_general(
+            rows, table_ref[...], (((0,), (0,)), ((), ())), preferred_element_type=jnp.float32
+        )
+
+    def early(*refs):
+        half = len(refs) // 2
         for t in range(latitudes):
-            value = None
-            for part_ref, table_ref in zip(part_refs, table_refs):
-                rows = part_ref[:, t].reshape(table_ref.shape[0], width)
-                term = lax.dot_general(
-                    rows, table_ref[...], (((0,), (0,)), ((), ())), preferred_element_type=jnp.float32
-                )
-                value = term if value is None else value + term
-            for tile in range(tiles):
-                total[pl.ds(tile * width * latitudes + t, width, stride=latitudes), :] = value[
+            value = term(refs[0], refs[half], t)
+            for part_ref, table_ref in zip(refs[1:half], refs[half + 1 : -1]):
+                value = value + term(part_ref, table_ref, t)
+            refs[-1][t] = value
+
+    def late(part_ref, table_ref, sum_ref, out_ref, total):
+        size = columns * latitudes
+        for t in range(latitudes):
+            value = sum_ref[t] + term(part_ref, table_ref, t)
+            for tile in range(width // 128):
+                total[pl.ds(tile * size + t, columns, stride=latitudes), :] = value[
                     :, tile * 128 : (tile + 1) * 128
                 ]
-        for tile in range(tiles):
+        for tile in range(width // 128):
             out_ref[:, :, tile * 128 : (tile + 1) * 128] = (
-                total[tile * width * latitudes : (tile + 1) * width * latitudes, :]
-                .reshape(width, latitudes, 128)
+                total[tile * size : (tile + 1) * size, :]
+                .reshape(columns, latitudes, 128)
                 .astype(jnp.bfloat16)
             )
 
+    def part_spec(part):
+        return pl.BlockSpec(part.shape, lambda n: (0, 0, 0, 0))
+
+    def table_spec(table):
+        return pl.BlockSpec((table.shape[0], width), lambda n: (0, n))
+
+    sum_spec = pl.BlockSpec((latitudes, columns, width), lambda n: (0, 0, n))
+    params = pltpu.CompilerParams(vmem_limit_bytes=VMEM_BYTES)
+    partial = pl.pallas_call(
+        early,
+        grid=(longitudes // width,),
+        in_specs=[*map(part_spec, parts[:-1]), *map(table_spec, tables[:-1])],
+        out_specs=sum_spec,
+        out_shape=jax.ShapeDtypeStruct((latitudes, columns, longitudes), jnp.float32),
+        compiler_params=params,
+        cost_estimate=pl.CostEstimate(
+            flops=2 * latitudes * columns * longitudes * sum(t.shape[0] for t in tables[:-1]),
+            bytes_accessed=4 * latitudes * columns * longitudes,
+            transcendentals=0,
+        ),
+    )(*parts[:-1], *tables[:-1])
     return pl.pallas_call(
-        kernel,
-        grid=(columns // width,),
-        in_specs=[
-            *[pl.BlockSpec((owners, latitudes, part.shape[2], width), lambda c: (0, 0, 0, c)) for part in parts],
-            *[pl.BlockSpec(table.shape, lambda c: (0, 0)) for table in tables],
-        ],
-        out_specs=pl.BlockSpec((width, latitudes, longitudes), lambda c: (c, 0, 0)),
+        late,
+        grid=(longitudes // width,),
+        in_specs=[part_spec(parts[-1]), table_spec(tables[-1]), sum_spec],
+        out_specs=pl.BlockSpec((columns, latitudes, width), lambda n: (0, 0, n)),
         out_shape=jax.ShapeDtypeStruct((columns, latitudes, longitudes), jnp.bfloat16),
-        scratch_shapes=[pltpu.VMEM((tiles * width * latitudes, 128), jnp.float32)],
-        compiler_params=pltpu.CompilerParams(vmem_limit_bytes=VMEM_BYTES),
-    )(*parts, *tables)
+        scratch_shapes=[pltpu.VMEM((width // 128 * columns * latitudes, 128), jnp.float32)],
+        compiler_params=params,
+    )(parts[-1], tables[-1], partial)
 
 
 def local(coefficients, rotations, legendre, degree_slot, column_order):
@@ -161,10 +185,12 @@
         mine = lax.dynamic_slice_in_dim(
             legendre, lax.axis_index("grp") * (latitudes // groups), latitudes // groups, axis=0
         )
-    mine = mine.reshape(mine.shape[0], buckets, owners, share, orders)
-    packed = jnp.concatenate([mine[:, b, :, :, slot_count * b :] for b in range(buckets)], axis=-1)
+    mine = mine.reshape(mine.shape[0], buckets, owners, share, orders).transpose(2, 0, 3, 1, 4)
+    mine = mine.reshape(owners, -1, buckets * orders)
+    packed = jnp.concatenate(
+        [mine[:, :, orders * b + slot_count * b : orders * (b + 1)] for b in range(buckets)], axis=-1
+    )
     lanes = packed.shape[-1]
-    packed = packed.transpose(1, 0, 2, 3).reshape(owners, -1, lanes)
     moved = lax.all_to_all(packed, "own", split_axis=0, concat_axis=0, tiled=True)
 
     degrees = lax.dynamic_slice_in_dim(degree_slot, own_index * slot_local, slot_local, axis=1)
@@ -200,8 +226,10 @@
     degree_ids = jnp.arange(slot_count, dtype=jnp.int32)
     permuters = (degree_ids[None, :, None] == degree_slot[:, None, :]).astype(jnp.bfloat16)
 
-    def synthesize(blocks):
+    def synthesize(blocks, received, after):
         pieces = []
+        if after is not None:
+            received, _ = lax.optimization_barrier((received, after))
         for block in blocks:
             start = slot_count * (block * buckets - block * (block - 1) // 2)
             count = buckets - block
@@ -214,7 +242,7 @@
             summed = jnp.einsum("tiks,ksipc->tipc", rows, values, preferred_element_type=jnp.float32)
             pieces.append(summed.astype(jnp.bfloat16).reshape(owners, latitudes, share * 2, columns))
         outgoing = jnp.concatenate(pieces, axis=2)
-        return lax.all_to_all(outgoing, "own", split_axis=0, concat_axis=0, tiled=True)
+        return outgoing, lax.all_to_all(outgoing, "own", split_axis=0, concat_axis=0, tiled=True)
 
     longitude = jnp.arange(longitudes, dtype=jnp.int32)
     low = buckets // 4
@@ -223,9 +251,10 @@
         list(range(low, high)),
         list(range(low)),
     ]
-    parts, tables = [], []
+    parts, tables, after = [], [], None
     for blocks in groups_of_blocks:
-        parts.append(synthesize(blocks))
+        after, part = synthesize(blocks, received, after if len(parts) == 2 else None)
+        parts.append(part)
         held = (
             slot_count * jnp.asarray(blocks, jnp.int32)[None, :, None]
             + share * jnp.arange(owners, dtype=jnp.int32)[:, None, None]

time: 543 us -> 547 us (level)
  local copies, waits for them, and re-layouts: 141 us -> 159 us
  waiting for transfers between devices: 243 us -> 229 us
    all_to_all x2, waiting for transfers between devices: 87 us -> 75.1 us  [local(): lax.all_to_all(outgoing, 'own', split_axis=0, concat_axis=0, tiled=True)]
    unnamed x74 -> x98, local copies, waits for them, and re-layouts: 40.4 us -> 52.1 us
    slice x14, local copies, waits for them, and re-layouts: 20.9 us -> 14.7 us  [synthesize(): rows = moved[:, :, start:start + slot_count * count]]
    pallas_call x1 -> x2, Pallas kernels: 23.9 us -> 27.1 us  [the longest x1 14.4 us: transform(): pl.pallas_call(late, grid=(longitudes // width,), in_specs=[part_spec(par...]
  transfers between devices with their start and end apart: 7 -> 7, of which waited for: 7 -> 6; matrix products, arithmetic and copies ran while one was open for 29% -> 30% of each run, Pallas kernels for 7% -> 9%
where the time goes in v2:
time: 547 us; the launch traced here: 539 us
  waiting for transfers between devices  229 us (42%)
  local copies, waits for them, and re-layouts  159 us (29%)
  Pallas kernels  63.8 us (12%)
  starting transfers between devices  33.2 us (6%)
  matrix products  22.3 us (4%)
  other arithmetic  17.3 us (3%)
  between operations  14.7 us (3%)
    all_to_all x3, waiting for transfers between devices, synthesize(): lax.all_to_all(outgoing, 'own', split_axis=0, concat_axis=0, tiled=True)  88.2 us
    all_to_all x2, waiting for transfers between devices, local(): lax.all_to_all(outgoing, 'own', split_axis=0, concat_axis=0, tiled=True)  75.1 us
    all_gather x1, waiting for transfers between devices, local(): moved = lax.all_gather(moved, 'grp', axis=0, tiled=False)  58.3 us
    unnamed x98, local copies, waits for them, and re-layouts  52.1 us
    pallas_call x2, Pallas kernels, rotate_classes(): pl.pallas_call(kernel, grid_spec=pltpu.PrefetchScalarGridSpec(num_scalar_...  36.7 us
    all_to_all x3, starting transfers between devices, synthesize(): lax.all_to_all(outgoing, 'own', split_axis=0, concat_axis=0, tiled=True)  16 us
    slice x16, local copies, waits for them, and re-layouts, local(): arrived[:, start:start + size]  15.3 us
    slice x14, local copies, waits for them, and re-layouts, synthesize(): rows = moved[:, :, start:start + slot_count * count]  14.7 us
  transfers between devices with their start and end apart: 7, of which 6 were waited for; matrix products, arithmetic and copies ran while one was open for 30% of the time, Pallas kernels for 9%

profile of v2, /device:TPU:13, one launch (start us, length us, event | category | flops | bytes accessed | tf_op | source)
XLA Modules:
  0.0 539.3 jit_solution(8071189756730752392)
XLA Ops:
  6.5 2.6 constant_dynamic-slice_fusion
  9.2 2.4 copy.267
  11.6 4.9 copy.196
  16.5 7.4 %reshape.619 = bf16[16,32,4096]{2,1,0:T(8,128)(2,1)} reshape(bf16[16,8,4,8,512]{4,3,2,1,0:T(8,128)(2,1)} %copy.196) | data formatting | bytes 8388608 | tf_op jit(solution)/shard_map/reshape | solution.py:189
  29.1 3.7 concatenate.20
  32.9 6.9 %all-to-all-start.2 = ((bf16[16,32,2304]{2,1,0:T(8,128)(2,1)}), bf16[16,32,2304]{2,1,0:T(8,128)(2,1)}, u32[]{:S(2)}, u32[]{:S(2)}) async-start(bf16[16,32,2304]{2,1,0:T(8,128)(2,1)} %concatenate.20), calls=%async_computation.2 | async-start | bytes 4718592 | tf_op jit(solution)/shard_map/all_to_all | solution.py:194
  39.8 8.1 %slice.234 = bf16[4,1048576]{1,0:T(4,128)(2,1)} slice(bf16[4,3342336]{1,0:T(4,128)(2,1)} %param.17), slice={[0:4], [2293760:3342336]} | slice | bytes 16777216 | tf_op jit(solution)/shard_map/slice | solution.py:66
  47.8 9.6 %copy.318 = bf16[1,4,1024,1024]{3,2,1,0:T(8,128)(2,1)} copy(bf16[1,4,1024,1024]{3,1,2,0:T(4,128)(2,1)} %bitcast.317) | data formatting | bytes 16777216
  57.5 3.6 copy.319
  62.4 20.2 %shard_map.155 = (bf16[4,1024,256]{2,1,0:T(8,128)(2,1)}, bf16[4,896,256]{2,1,0:T(8,128)(2,1)}) custom-call(s32[8,4]{1,0:T(8,128)} %dynamic-slice_add_fusion.degree_ref, bf16[4,256,4608]{2,1,0:T(8,128)(2,1)} %coef_ref.3, bf16[256,256]{1,0:T(8,128)(2,1)} %fusion.81.pick_ref, bf16[4,1024,1024]{2,1,0:T(8,128)(2,1)} %bitcast.338, bf16[4,896,896]{2,1,0:T(8,128)(2,1)} %bitcast.348, ...), custom_call_target="tpu_custom_call" | custom-call | flops 7583301632 | bytes 22675456 | tf_op jit(solution)/shard_map/pallas_call | solution.py:71
  82.6 3.6 copy_bitcast_fusion.4
  86.2 6.6 %all-to-all-done.2 = bf16[16,32,2304]{2,1,0:T(8,128)(2,1)} async-done(((bf16[16,32,2304]{2,1,0:T(8,128)(2,1)}), bf16[16,32,2304]{2,1,0:T(8,128)(2,1)}, u32[]{:S(2)}, u32[]{:S(2)}) %all-to-all-start.2) | async-done | bytes 2359328 | tf_op jit(solution)/shard_map/all_to_all | solution.py:194
  92.8 4.9 all-to-all-start.1
  100.0 2.8 copy.321
  110.4 16.5 %shard_map.154 = (bf16[4,768,256]{2,1,0:T(8,128)(2,1)}, bf16[4,640,256]{2,1,0:T(8,128)(2,1)}, bf16[4,512,256]{2,1,0:T(8,128)(2,1)}, bf16[4,384,256]{2,1,0:T(8,12...) custom-call(s32[8,4]{1,0:T(8,128)} %dynamic-slice_add_fusion.degree_ref, ...), custom_call_target="tpu_custom_call" | custom-call | flops 6106906624 | bytes 22937600 | tf_op jit(solution)/shard_map/pallas_call | solution.py:71
  130.8 3.0 copy.320
  133.8 50.7 %all-to-all-done.1 = bf16[16,4,120,256]{3,2,1,0:T(8,128)(2,1)} async-done(((bf16[16,4,120,256]{3,2,1,0:T(8,128)(2,1)}), bf16[16,4,120,256]{3,2,1,0:T(8,128)(2,1)}, u32[]{:S(2)}, u32[]{:S(2)}) %all-to-all-start.1) | async-done | bytes 3932192 | tf_op jit(solution)/shard_map/all_to_all | solution.py:211
  184.5 4.9 all-to-all-start
  196.7 58.3 %all-gather.3.cloned.1.call-done = bf16[32,32,2304]{2,1,0:T(8,128)(2,1)} async-done(((bf16[16,32,2304]{2,1,0:T(8,128)(2,1)}), bf16[32,32,2304]{2,1,0:T(8,128)(2,1)}) %all-gather.3.cloned.1.call-update) | async-done | bytes 4718608 | tf_op jit(solution)/shard_map/all_gather | solution.py:222
  255.1 4.9 copy.197
  260.0 2.6 copy.198
  285.5 24.4 %all-to-all-done = bf16[16,4,168,256]{3,2,1,0:T(8,128)(2,1)} async-done(((bf16[16,4,168,256]{3,2,1,0:T(8,128)(2,1)}), bf16[16,4,168,256]{3,2,1,0:T(8,128)(2,1)}, u32[]{:S(2)}, u32[]{:S(2)}) %all-to-all-start) | async-done | bytes 5505056 | tf_op jit(solution)/shard_map/all_to_all | solution.py:211
  310.0 4.9 all-to-all-start.4
  354.3 3.7 bitcast_convert_fusion.6
  358.0 2.9 copy_dynamic-update-slice_fusion
  365.5 6.0 %all-to-all-start.5 = ((bf16[16,16,32,256]{3,2,1,0:T(8,128)(2,1)}), bf16[16,16,32,256]{3,2,1,0:T(8,128)(2,1)}, u32[]{:S(2)}, u32[]{:S(2)}) async-start(bf16[16,16,32,256]{3,2,1,0:T(8,128)(2,1)} %constant_dynamic-update-slice_fusion.5), calls=%async_computation.5 | async-start | bytes 8388608 | tf_op jit(solution)/shard_map/all_to_all | solution.py:245
  394.9 69.1 %all-to-all-done.5.refs_1_ = bf16[16,16,32,256]{3,2,1,0:T(8,128)(2,1)} async-done(((bf16[16,16,32,256]{3,2,1,0:T(8,128)(2,1)}), bf16[16,16,32,256]{3,2,1,0:T(8,128)(2,1)}, u32[]{:S(2)}, u32[]{:S(2)}) %all-to-all-start.5) | async-done | bytes 4194336 | tf_op jit(solution)/shard_map/all_to_all | solution.py:245
  464.0 5.1 all-to-all-start.3
  477.4 4.2 fusion.55
  484.4 12.7 %shard_map.156.sum_ref = f32[16,256,1024]{2,1,0:T(8,128)} custom-call(bf16[16,16,16,256]{3,2,1,0:T(8,128)(2,1)} %copy-done.2, bf16[16,16,32,256]{3,2,1,0:T(8,128)(2,1)} %all-to-all-done.5.refs_1_, bf16[256,1024]{1,0:T(8,128)(2,1)} %convert_element_type.205.refs_2_, bf16[512,1024]{1,0:T(8,128)(2,1)} %convert_element_type.208.refs_3_), custom_call_target="tpu_custom_call" | custom-call | flops 6442450944 | bytes 16777216 | tf_op jit(solution)/shard_map/pallas_call | solution.py:147
  497.1 19.2 %all-to-all-done.3.part_ref = bf16[16,16,16,256]{3,2,1,0:T(8,128)(2,1)S(1)} async-done(((bf16[16,16,16,256]{3,2,1,0:T(8,128)(2,1)}), bf16[16,16,16,256]{3,2,1,0:T(8,128)(2,1)S(1)}, u32[]{:S(2)}, u32[]{:S(2)}) %all-to-all-start.3) | async-done | bytes 2097184 | tf_op jit(solution)/shard_map/all_to_all | solution.py:245
  517.6 14.4 %shard_map.157 = bf16[256,16,1024]{2,1,0:T(8,128)(2,1)} custom-call(bf16[16,16,16,256]{3,2,1,0:T(8,128)(2,1)} %copy-done.4, bf16[256,1024]{1,0:T(8,128)(2,1)} %convert_element_type.193.table_ref, f32[16,256,1024]{2,1,0:T(8,128)} %shard_map.156.sum_ref), custom_call_target="tpu_custom_call" | custom-call | tf_op jit(solution)/shard_map/pallas_call | solution.py:160
  (213 shorter events, 129.8 us)
Async XLA Ops:
  23.8 5.1 copy-start.1
  23.8 5.3 slice-start.6
  23.8 5.3 slice-start.7
  32.9 59.9 %all-to-all-start.2 = ((bf16[16,32,2304]{2,1,0:T(8,128)(2,1)}), bf16[16,32,2304]{2,1,0:T(8,128)(2,1)}, u32[]{:S(2)}, u32[]{:S(2)}) async-start(bf16[16,32,2304]{2,1,0:T(8,128)(2,1)} %concatenate.20), calls=%async_computation.2 | async-start | bytes 4718592 | tf_op jit(solution)/shard_map/all_to_all | solution.py:194
  47.8 9.6 %slice-start = ((bf16[4,3342336]{1,0:T(4,128)(2,1)}), bf16[4,802816]{1,0:T(4,128)(2,1)S(1)}, s32[]{:S(2)}) async-start(bf16[4,3342336]{1,0:T(4,128)(2,1)} %param.17), calls=%async_computation.7 | async-start | bytes 12845056 | tf_op jit(solution)/shard_map/slice | solution.py:66
  57.5 3.6 copy-start.27
  57.5 4.2 copy-start.29
  92.8 91.7 %all-to-all-start.1 = ((bf16[16,4,120,256]{3,2,1,0:T(8,128)(2,1)}), bf16[16,4,120,256]{3,2,1,0:T(8,128)(2,1)}, u32[]{:S(2)}, u32[]{:S(2)}) async-start(bf16[16,4,120,256]{3,2,1,0:T(8,128)(2,1)} %copy_bitcast_fusion.4), calls=%async_computation.1 | async-start | bytes 7864320 | tf_op jit(solution)/shard_map/all_to_all | solution.py:211
  97.7 2.3 slice-start.1
  100.0 2.9 slice-start.2
  102.9 2.1 slice-start.3
  104.9 1.7 slice-start.4
  126.8 1.8 copy-start.18
  184.5 125.5 %all-to-all-start = ((bf16[16,4,168,256]{3,2,1,0:T(8,128)(2,1)}), bf16[16,4,168,256]{3,2,1,0:T(8,128)(2,1)}, u32[]{:S(2)}, u32[]{:S(2)}) async-start(bf16[16,4,168,256]{3,2,1,0:T(8,128)(2,1)} %bitcast.324), calls=%async_computation | async-start | bytes 11010048 | tf_op jit(solution)/shard_map/all_to_all | solution.py:211
  189.4 65.6 %all-gather.3.cloned.1.call-start = ((), (), s32[]{:S(2)}) async-start(), calls=%async_computation.6 | async-start | bytes 7077888 | tf_op jit(solution)/shard_map/all_gather | solution.py:222
  190.3 85.3 %copy-start.16 = (pred[8,64,64]{1,2,0:T(32,128)(4,1)}, pred[8,64,64]{1,2,0:T(32,128)(4,1)S(1)}, u32[]{:S(2)}) copy-start(pred[8,64,64]{1,2,0:T(32,128)(4,1)S(1)} %iota_compare_fusion) | copy-start | bytes 98308
  195.3 77.4 %copy-start.3 = (bf16[64,64,256]{2,0,1:T(8,128)(2,1)}, bf16[64,64,256]{2,0,1:T(8,128)(2,1)S(1)}, u32[]{:S(2)}) copy-start(bf16[64,64,256]{2,0,1:T(8,128)(2,1)S(1)} %copy.189) | copy-start | bytes 6291460
  262.6 2.9 copy-start
  272.8 3.0 copy-start.19
  276.4 1.7 copy-start.15
  278.1 4.0 copy-start.13
  310.0 54.1 %all-to-all-start.4 = ((bf16[16,16,16,256]{3,2,1,0:T(8,128)(2,1)}), bf16[16,16,16,256]{3,2,1,0:T(8,128)(2,1)S(1)}, u32[]{:S(2)}, u32[]{:S(2)}) async-start(bf16[16,16,16,256]{3,2,1,0:T(8,128)(2,1)} %pad_maximum_fusion.2), calls=%async_computation.4 | async-start | bytes 4194304 | tf_op jit(solution)/shard_map/all_to_all | solution.py:245
  322.9 3.1 copy-start.14
  345.2 9.1 %copy-start.17 = (pred[8,64,64]{1,2,0:T(32,128)(4,1)S(1)}, pred[8,64,64]{1,2,0:T(32,128)(4,1)}, u32[]{:S(2)}) copy-start(pred[8,64,64]{1,2,0:T(32,128)(4,1)} %copy-done.16) | copy-start | bytes 98308
  358.0 2.9 copy-start.9
  358.0 4.0 copy-start.10
  360.9 2.1 copy-start.11
  365.5 98.5 %all-to-all-start.5 = ((bf16[16,16,32,256]{3,2,1,0:T(8,128)(2,1)}), bf16[16,16,32,256]{3,2,1,0:T(8,128)(2,1)}, u32[]{:S(2)}, u32[]{:S(2)}) async-start(bf16[16,16,32,256]{3,2,1,0:T(8,128)(2,1)} %constant_dynamic-update-slice_fusion.5), calls=%async_computation.5 | async-start | bytes 8388608 | tf_op jit(solution)/shard_map/all_to_all | solution.py:245
  387.9 1.5 copy-start.21
  394.9 74.2 %copy-start.31 = (s32[2]{0:T(128)S(1)}, s32[2]{0:T(128)}, u32[]{:S(2)}) copy-start(s32[2]{0:T(128)} %constant.93) | copy-start | bytes 28
  464.0 52.3 %all-to-all-start.3 = ((bf16[16,16,16,256]{3,2,1,0:T(8,128)(2,1)}), bf16[16,16,16,256]{3,2,1,0:T(8,128)(2,1)S(1)}, u32[]{:S(2)}, u32[]{:S(2)}) async-start(bf16[16,16,16,256]{3,2,1,0:T(8,128)(2,1)} %pad_maximum_fusion.1), calls=%async_computation.3 | async-start | bytes 4194304 | tf_op jit(solution)/shard_map/all_to_all | solution.py:245
  475.4 1.7 copy-start.30
  (15 other events, 18.8 us)
Sparse Core Ops, SparseCore 0:
  191.8 63.2 all-gather.2

commit v3 on v2

--- a/solution.py
+++ b/solution.py
@@ -185,12 +185,10 @@
         mine = lax.dynamic_slice_in_dim(
             legendre, lax.axis_index("grp") * (latitudes // groups), latitudes // groups, axis=0
         )
-    mine = mine.reshape(mine.shape[0], buckets, owners, share, orders).transpose(2, 0, 3, 1, 4)
-    mine = mine.reshape(owners, -1, buckets * orders)
-    packed = jnp.concatenate(
-        [mine[:, :, orders * b + slot_count * b : orders * (b + 1)] for b in range(buckets)], axis=-1
-    )
+    mine = mine.reshape(mine.shape[0], buckets, owners, share, orders)
+    packed = jnp.concatenate([mine[:, b, :, :, slot_count * b :] for b in range(buckets)], axis=-1)
     lanes = packed.shape[-1]
+    packed = packed.transpose(1, 0, 2, 3).reshape(owners, -1, lanes)
     moved = lax.all_to_all(packed, "own", split_axis=0, concat_axis=0, tiled=True)
 
     degrees = lax.dynamic_slice_in_dim(degree_slot, own_index * slot_local, slot_local, axis=1)
@@ -208,6 +206,7 @@
         outgoing = jnp.concatenate(
             [part.reshape(slot_local, owners, -1, columns) for part in rotated], axis=2
         ).transpose(1, 0, 2, 3)
+        degrees, _ = lax.optimization_barrier((degrees, outgoing))
         arrived = lax.all_to_all(outgoing, "own", split_axis=0, concat_axis=0, tiled=True)
         arrived = arrived.reshape(owners * slot_local, -1, columns)
         start = 0
@@ -223,23 +222,34 @@
         moved = moved.reshape(groups, owners, latitudes // groups, share, lanes)
         moved = moved.transpose(1, 0, 2, 3, 4)
     moved = moved.reshape(owners * latitudes, share, lanes)
-    degree_ids = jnp.arange(slot_count, dtype=jnp.int32)
-    permuters = (degree_ids[None, :, None] == degree_slot[:, None, :]).astype(jnp.bfloat16)
+    held_degrees = degree_slot + slot_count * jnp.arange(buckets, dtype=jnp.int32)[:, None]
+    permuter = jnp.arange(orders, dtype=jnp.int32)[:, None] == held_degrees.reshape(1, -1)
+    permuter = permuter.astype(jnp.bfloat16)
+    tables_of_blocks = []
+    for block in range(buckets):
+        start = slot_count * (block * buckets - block * (block - 1) // 2)
+        first = slot_count * block
+        rows = jnp.einsum(
+            "til,lj->itj",
+            moved[:, :, start : start + orders - first],
+            permuter[first:, first:],
+            preferred_element_type=jnp.float32,
+        )
+        tables_of_blocks.append(rows.astype(jnp.bfloat16))
+    low_arrived = {k: received[k] for k in chunks[1]}
+    low_arrived, tables_of_blocks[:high] = lax.optimization_barrier(
+        (low_arrived, tables_of_blocks[:high])
+    )
 
     def synthesize(blocks, received, after):
         pieces = []
         if after is not None:
             received, _ = lax.optimization_barrier((received, after))
         for block in blocks:
-            start = slot_count * (block * buckets - block * (block - 1) // 2)
-            count = buckets - block
-            rows = moved[:, :, start : start + slot_count * count]
-            rows = rows.reshape(owners * latitudes, share, count, slot_count)
-            rows = jnp.einsum(
-                "tikl,kls->tiks", rows, permuters[block:], preferred_element_type=jnp.float32
-            ).astype(jnp.bfloat16)
-            values = jnp.stack([received[k][:, block] for k in range(block, buckets)], axis=0)
-            summed = jnp.einsum("tiks,ksipc->tipc", rows, values, preferred_element_type=jnp.float32)
+            values = jnp.concatenate([received[k][:, block] for k in range(block, buckets)], axis=0)
+            summed = jnp.einsum(
+                "itj,jipc->tipc", tables_of_blocks[block], values, preferred_element_type=jnp.float32
+            )
             pieces.append(summed.astype(jnp.bfloat16).reshape(owners, latitudes, share * 2, columns))
         outgoing = jnp.concatenate(pieces, axis=2)
         return outgoing, lax.all_to_all(outgoing, "own", split_axis=0, concat_axis=0, tiled=True)
@@ -252,6 +262,7 @@
         list(range(low)),
     ]
     parts, tables, after = [], [], None
+    received = {**received, **low_arrived}
     for blocks in groups_of_blocks:
         after, part = synthesize(blocks, received, after if len(parts) == 2 else None)
         parts.append(part)

time: 547 us -> 533 us (0.974)
  local copies, waits for them, and re-layouts: 159 us -> 115 us
  waiting for transfers between devices: 229 us -> 266 us
  matrix products: 22.3 us -> 16.7 us
    all_to_all x3, waiting for transfers between devices: 88.2 us -> 124 us  [synthesize(): lax.all_to_all(outgoing, 'own', split_axis=0, concat_axis=0, tiled=True)]
    slice x24 -> x0, local copies, waits for them, and re-layouts: 19.9 us -> none  [the longest x14 14.7 us: synthesize(): rows = moved[:, :, start:start + slot_count * count]]
    convert_element_type x6 -> x0, local copies, waits for them, and re-layouts: 9.56 us -> none  [synthesize(): summed.astype(jnp.bfloat16).reshape(owners, latitudes, share * 2, columns)]
    another operation x5 -> x0, local copies, waits for them, and re-layouts: 6.82 us -> none  [synthesize(): jnp.stack([received[k][:, block] for k in range(block, buckets)], axis=0)]
    reshape x7 -> x4, local copies, waits for them, and re-layouts: 8.72 us -> 2.34 us  [synthesize(): summed.astype(jnp.bfloat16).reshape(owners, latitudes, share * 2, columns)]
    squeeze x0 -> x10, local copies, waits for them, and re-layouts: none -> 5.66 us  [the longest x8 4.45 us: local(): mine[:, b, :, :, slot_count * b:]]
    dot_general x14, matrix products: 22.3 us -> 16.7 us  [the longest x6 9.12 us: local(): jnp.einsum('til,lj->itj', moved[:, :, start:start + orders - first], perm...]
    unnamed x98 -> x88, local copies, waits for them, and re-layouts: 52.1 us -> 46.7 us
  transfers between devices with their start and end apart: 7 -> 7, of which waited for: 6 -> 7; matrix products, arithmetic and copies ran while one was open for 30% -> 23% of each run, Pallas kernels for 9% -> 9%
where the time goes in v3:
time: 533 us; the launch traced here: 527 us
  waiting for transfers between devices  266 us (50%)
  local copies, waits for them, and re-layouts  115 us (22%)
  Pallas kernels  63.7 us (12%)
  starting transfers between devices  32.4 us (6%)
  other arithmetic  18.3 us (3%)
  matrix products  16.7 us (3%)
  between operations  14.4 us (3%)
    all_to_all x3, waiting for transfers between devices, synthesize(): lax.all_to_all(outgoing, 'own', split_axis=0, concat_axis=0, tiled=True)  124 us
    all_to_all x2, waiting for transfers between devices, local(): lax.all_to_all(outgoing, 'own', split_axis=0, concat_axis=0, tiled=True)  79.3 us
    all_gather x1, waiting for transfers between devices, local(): moved = lax.all_gather(moved, 'grp', axis=0, tiled=False)  56.1 us
    unnamed x88, local copies, waits for them, and re-layouts  46.7 us
    pallas_call x2, Pallas kernels, rotate_classes(): pl.pallas_call(kernel, grid_spec=pltpu.PrefetchScalarGridSpec(num_scalar_...  36.6 us
    slice x16, local copies, waits for them, and re-layouts, local(): arrived[:, start:start + size]  15.8 us
    all_to_all x3, starting transfers between devices, synthesize(): lax.all_to_all(outgoing, 'own', split_axis=0, concat_axis=0, tiled=True)  14.9 us
    pallas_call x1, Pallas kernels, transform(): pl.pallas_call(late, grid=(longitudes // width,), in_specs=[part_spec(par...  14.4 us
  transfers between devices with their start and end apart: 7, of which 7 were waited for; matrix products, arithmetic and copies ran while one was open for 23% of the time, Pallas kernels for 9%

profile of v3, /device:TPU:13, one launch (start us, length us, event | category | flops | bytes accessed | tf_op | source)
XLA Modules:
  0.0 526.7 jit_solution(4375282363524227850)
XLA Ops:
  6.5 2.6 constant_dynamic-slice_fusion
  9.2 2.4 copy.204
  16.0 3.7 concatenate.41
  23.2 6.9 %all-to-all-start.1 = ((bf16[16,32,2304]{2,1,0:T(8,128)(2,1)}), bf16[16,32,2304]{2,1,0:T(8,128)(2,1)}, u32[]{:S(2)}, u32[]{:S(2)}) async-start(bf16[16,32,2304]{2,1,0:T(8,128)(2,1)} %copy.150), calls=%async_computation.1 | async-start | bytes 4718592 | tf_op jit(solution)/shard_map/all_to_all | solution.py:192
  30.0 8.1 %slice.222 = bf16[4,1048576]{1,0:T(4,128)(2,1)} slice(bf16[4,3342336]{1,0:T(4,128)(2,1)} %param.17), slice={[0:4], [2293760:3342336]} | slice | bytes 16777216 | tf_op jit(solution)/shard_map/slice | solution.py:66
  38.1 9.8 %copy.227 = bf16[1,4,1024,1024]{3,2,1,0:T(8,128)(2,1)} copy(bf16[1,4,1024,1024]{3,1,2,0:T(4,128)(2,1)} %bitcast.273) | data formatting | bytes 16777216
  47.9 3.6 copy.228
  52.8 20.2 %shard_map.154 = (bf16[4,1024,256]{2,1,0:T(8,128)(2,1)}, bf16[4,896,256]{2,1,0:T(8,128)(2,1)}) custom-call(s32[8,4]{1,0:T(8,128)} %dynamic-slice_add_fusion.degree_ref, bf16[4,256,4608]{2,1,0:T(8,128)(2,1)} %coef_ref.3, bf16[256,256]{1,0:T(8,128)(2,1)} %fusion.71.pick_ref, bf16[4,1024,1024]{2,1,0:T(8,128)(2,1)} %bitcast.302, bf16[4,896,896]{2,1,0:T(8,128)(2,1)} %bitcast.310, ...), custom_call_target="tpu_custom_call" | custom-call | flops 7583301632 | bytes 22675456 | tf_op jit(solution)/shard_map/pallas_call | solution.py:71
  73.0 3.6 copy_bitcast_fusion.4
  76.6 6.5 %all-to-all-done.1 = bf16[16,32,2304]{2,1,0:T(8,128)(2,1)} async-done(((bf16[16,32,2304]{2,1,0:T(8,128)(2,1)}), bf16[16,32,2304]{2,1,0:T(8,128)(2,1)}, u32[]{:S(2)}, u32[]{:S(2)}) %all-to-all-start.1) | async-done | bytes 2359328 | tf_op jit(solution)/shard_map/all_to_all | solution.py:192
  83.0 5.2 all-to-all-start.2
  88.3 2.3 slice-done.1
  90.6 2.8 copy.230
  101.0 16.4 %shard_map.155 = (bf16[4,768,256]{2,1,0:T(8,128)(2,1)}, bf16[4,640,256]{2,1,0:T(8,128)(2,1)}, bf16[4,512,256]{2,1,0:T(8,128)(2,1)}, bf16[4,384,256]{2,1,0:T(8,12...) custom-call(s32[8,4]{1,0:T(8,128)} %dynamic-slice_add_fusion.degree_ref, ...), custom_call_target="tpu_custom_call" | custom-call | flops 6106906624 | bytes 22937600 | tf_op jit(solution)/shard_map/pallas_call | solution.py:71
  121.4 3.0 copy.229
  124.5 50.5 %all-to-all-done.2 = bf16[16,4,120,256]{3,2,1,0:T(8,128)(2,1)} async-done(((bf16[16,4,120,256]{3,2,1,0:T(8,128)(2,1)}), bf16[16,4,120,256]{3,2,1,0:T(8,128)(2,1)}, u32[]{:S(2)}, u32[]{:S(2)}) %all-to-all-start.2) | async-done | bytes 3932192 | tf_op jit(solution)/shard_map/all_to_all | solution.py:210
  175.0 4.9 all-to-all-start
  180.3 4.4 copy.151
  192.0 56.1 %all-gather.3.cloned.1.call-done = bf16[32,32,2304]{2,0,1:T(8,128)(2,1)} async-done(((bf16[16,32,2304]{2,0,1:T(8,128)(2,1)}), bf16[32,32,2304]{2,0,1:T(8,128)(2,1)}) %all-gather.3.cloned.1.call-update) | async-done | bytes 4718608 | tf_op jit(solution)/shard_map/all_gather | solution.py:221
  248.1 7.1 %copy.152 = bf16[16,2,8,4,2304]{4,2,1,0,3:T(8,128)(2,1)} copy(bf16[16,2,8,4,2304]{4,0,1,3,2:T(8,128)(2,1)} %bitcast.318) | data formatting | bytes 9437184 | tf_op jit(solution)/shard_map/transpose | solution.py:223
  271.7 28.7 %all-to-all-done = bf16[16,4,168,256]{3,2,1,0:T(8,128)(2,1)} async-done(((bf16[16,4,168,256]{3,2,1,0:T(8,128)(2,1)}), bf16[16,4,168,256]{3,2,1,0:T(8,128)(2,1)}, u32[]{:S(2)}, u32[]{:S(2)}) %all-to-all-start) | async-done | bytes 5505056 | tf_op jit(solution)/shard_map/all_to_all | solution.py:210
  300.4 4.9 all-to-all-start.4
  329.1 23.7 %all-to-all-done.4.refs_0_ = bf16[16,16,16,256]{3,2,1,0:T(8,128)(2,1)S(1)} async-done(((bf16[16,16,16,256]{3,2,1,0:T(8,128)(2,1)}), bf16[16,16,16,256]{3,2,1,0:T(8,128)(2,1)S(1)}, u32[]{:S(2)}, u32[]{:S(2)}) %all-to-all-start.4) | async-done | bytes 2097184 | tf_op jit(solution)/shard_map/all_to_all | solution.py:255
  354.2 4.9 all-to-all-start.5
  370.0 81.5 %all-to-all-done.5.refs_1_ = bf16[16,16,32,256]{3,2,1,0:T(8,128)(2,1)} async-done(((bf16[16,16,32,256]{3,2,1,0:T(8,128)(2,1)}), bf16[16,16,32,256]{3,2,1,0:T(8,128)(2,1)}, u32[]{:S(2)}, u32[]{:S(2)}) %all-to-all-start.5) | async-done | bytes 4194336 | tf_op jit(solution)/shard_map/all_to_all | solution.py:255
  451.5 5.1 all-to-all-start.3
  457.0 2.1 fusion.70
  460.9 2.1 fusion.68
  464.9 4.2 fusion.51
  471.9 12.7 %shard_map.156.sum_ref = f32[16,256,1024]{2,1,0:T(8,128)} custom-call(bf16[16,16,16,256]{3,2,1,0:T(8,128)(2,1)} %copy-done, bf16[16,16,32,256]{3,2,1,0:T(8,128)(2,1)} %all-to-all-done.5.refs_1_, bf16[256,1024]{1,0:T(8,128)(2,1)} %convert_element_type.201.refs_2_, bf16[512,1024]{1,0:T(8,128)(2,1)} %convert_element_type.204.refs_3_), custom_call_target="tpu_custom_call" | custom-call | flops 6442450944 | bytes 16777216 | tf_op jit(solution)/shard_map/pallas_call | solution.py:147
  484.7 19.2 %all-to-all-done.3.part_ref = bf16[16,16,16,256]{3,2,1,0:T(8,128)(2,1)S(1)} async-done(((bf16[16,16,16,256]{3,2,1,0:T(8,128)(2,1)}), bf16[16,16,16,256]{3,2,1,0:T(8,128)(2,1)S(1)}, u32[]{:S(2)}, u32[]{:S(2)}) %all-to-all-start.3) | async-done | bytes 2097184 | tf_op jit(solution)/shard_map/all_to_all | solution.py:255
  505.2 14.4 %shard_map.157 = bf16[256,16,1024]{2,1,0:T(8,128)(2,1)} custom-call(bf16[16,16,16,256]{3,2,1,0:T(8,128)(2,1)} %copy-done.3, bf16[256,1024]{1,0:T(8,128)(2,1)} %convert_element_type.190.table_ref, f32[16,256,1024]{2,1,0:T(8,128)} %shard_map.156.sum_ref), custom_call_target="tpu_custom_call" | custom-call | tf_op jit(solution)/shard_map/pallas_call | solution.py:160
  (173 shorter events, 88.6 us)
Async XLA Ops:
  23.2 59.9 %all-to-all-start.1 = ((bf16[16,32,2304]{2,1,0:T(8,128)(2,1)}), bf16[16,32,2304]{2,1,0:T(8,128)(2,1)}, u32[]{:S(2)}, u32[]{:S(2)}) async-start(bf16[16,32,2304]{2,1,0:T(8,128)(2,1)} %copy.150), calls=%async_computation.1 | async-start | bytes 4718592 | tf_op jit(solution)/shard_map/all_to_all | solution.py:192
  38.1 9.8 %slice-start = ((bf16[4,3342336]{1,0:T(4,128)(2,1)}), bf16[4,802816]{1,0:T(4,128)(2,1)S(1)}, s32[]{:S(2)}) async-start(bf16[4,3342336]{1,0:T(4,128)(2,1)} %param.17), calls=%async_computation.7 | async-start | bytes 12845056 | tf_op jit(solution)/shard_map/slice | solution.py:66
  47.9 3.6 copy-start.25
  47.9 4.2 copy-start.26
  83.0 92.0 %all-to-all-start.2 = ((bf16[16,4,120,256]{3,2,1,0:T(8,128)(2,1)}), bf16[16,4,120,256]{3,2,1,0:T(8,128)(2,1)}, u32[]{:S(2)}, u32[]{:S(2)}) async-start(bf16[16,4,120,256]{3,2,1,0:T(8,128)(2,1)} %copy_bitcast_fusion.4), calls=%async_computation.2 | async-start | bytes 7864320 | tf_op jit(solution)/shard_map/all_to_all | solution.py:210
  88.3 2.3 slice-start.1
  90.6 2.9 slice-start.2
  93.5 2.1 slice-start.3
  95.6 1.8 slice-start.4
  117.5 1.8 copy-start.9
  119.3 1.3 copy-start.13
  119.4 1.4 copy-start.18
  175.0 125.4 %all-to-all-start = ((bf16[16,4,168,256]{3,2,1,0:T(8,128)(2,1)}), bf16[16,4,168,256]{3,2,1,0:T(8,128)(2,1)}, u32[]{:S(2)}, u32[]{:S(2)}) async-start(bf16[16,4,168,256]{3,2,1,0:T(8,128)(2,1)} %bitcast.280), calls=%async_computation | async-start | bytes 11010048 | tf_op jit(solution)/shard_map/all_to_all | solution.py:210
  179.9 68.2 %all-gather.3.cloned.1.call-start = ((), (), s32[]{:S(2)}) async-start(), calls=%async_computation.6 | async-start | bytes 7077888 | tf_op jit(solution)/shard_map/all_gather | solution.py:221
  190.8 64.4 %copy-start.2 = (bf16[64,64,256]{2,0,1:T(8,128)(2,1)}, bf16[64,64,256]{2,0,1:T(8,128)(2,1)S(1)}, u32[]{:S(2)}) copy-start(bf16[64,64,256]{2,0,1:T(8,128)(2,1)S(1)} %copy.157) | copy-start | bytes 6291460
  259.3 3.1 copy-start.1
  259.9 2.7 copy-start.16
  300.4 52.3 %all-to-all-start.4 = ((bf16[16,16,16,256]{3,2,1,0:T(8,128)(2,1)}), bf16[16,16,16,256]{3,2,1,0:T(8,128)(2,1)S(1)}, u32[]{:S(2)}, u32[]{:S(2)}) async-start(bf16[16,16,16,256]{3,2,1,0:T(8,128)(2,1)} %pad_maximum_fusion.2), calls=%async_computation.4 | async-start | bytes 4194304 | tf_op jit(solution)/shard_map/all_to_all | solution.py:255
  314.8 1.5 copy-start.8
  316.3 2.8 copy-start.5
  316.5 2.6 copy-start.19
  316.5 2.6 copy-start.22
  316.5 2.6 copy-start.23
  321.3 2.3 copy-start.15
  352.8 1.4 copy-start
  354.2 97.4 %all-to-all-start.5 = ((bf16[16,16,32,256]{3,2,1,0:T(8,128)(2,1)}), bf16[16,16,32,256]{3,2,1,0:T(8,128)(2,1)}, u32[]{:S(2)}, u32[]{:S(2)}) async-start(bf16[16,16,32,256]{3,2,1,0:T(8,128)(2,1)} %copy_dynamic-update-slice_fusion), calls=%async_computation.5 | async-start | bytes 8388608 | tf_op jit(solution)/shard_map/all_to_all | solution.py:255
  359.1 3.2 copy-start.7
  362.4 3.4 copy-start.12
  365.7 1.4 copy-start.11
  370.0 86.7 %copy-start.28 = (s32[2]{0:T(128)S(1)}, s32[2]{0:T(128)}, u32[]{:S(2)}) copy-start(s32[2]{0:T(128)} %constant.93) | copy-start | bytes 28
  451.5 52.3 %all-to-all-start.3 = ((bf16[16,16,16,256]{3,2,1,0:T(8,128)(2,1)}), bf16[16,16,16,256]{3,2,1,0:T(8,128)(2,1)S(1)}, u32[]{:S(2)}, u32[]{:S(2)}) async-start(bf16[16,16,16,256]{3,2,1,0:T(8,128)(2,1)} %pad_maximum_fusion.1), calls=%async_computation.3 | async-start | bytes 4194304 | tf_op jit(solution)/shard_map/all_to_all | solution.py:255
  463.0 1.7 copy-start.27
  (10 other events, 11.5 us)
Sparse Core Ops, SparseCore 0:
  184.8 63.2 all-gather.2

commit v4 on v3

--- a/solution.py
+++ b/solution.py
@@ -168,6 +168,40 @@
     )(parts[-1], tables[-1], partial)
 
 
+def pack(legendre, buckets, slot_count, owners, groups):
+    share = slot_count // owners
+    orders = slot_count * buckets
+    latitudes = legendre.shape[0] // groups
+    group = lax.axis_index("grp") if groups > 1 else jnp.int32(0)
+    starts = [slot_count * (b * buckets - b * (b - 1) // 2) for b in range(buckets + 1)]
+    lanes = starts[-1]
+    if share % 4:
+        mine = lax.dynamic_slice_in_dim(legendre, group * latitudes, latitudes, axis=0)
+        mine = mine.reshape(latitudes, buckets, owners, share, orders)
+        packed = jnp.concatenate([mine[:, b, :, :, slot_count * b :] for b in range(buckets)], axis=-1)
+        return packed.transpose(1, 0, 2, 3)
+
+    def kernel(_, in_ref, out_ref):
+        pieces = [
+            in_ref[0, slot_count * b : slot_count * (b + 1), slot_count * b :] for b in range(buckets)
+        ]
+        rows = jnp.concatenate(pieces, axis=-1)
+        for owner in range(owners):
+            out_ref[owner, 0] = rows[owner * share : (owner + 1) * share]
+
+    return pl.pallas_call(
+        kernel,
+        grid_spec=pltpu.PrefetchScalarGridSpec(
+            num_scalar_prefetch=1,
+            grid=(latitudes,),
+            in_specs=[pl.BlockSpec((1, orders, orders), lambda t, g: (g[0] + t, 0, 0))],
+            out_specs=pl.BlockSpec((owners, 1, share, lanes), lambda t, g: (0, t, 0, 0)),
+        ),
+        out_shape=jax.ShapeDtypeStruct((owners, latitudes, share, lanes), jnp.bfloat16),
+        compiler_params=pltpu.CompilerParams(vmem_limit_bytes=VMEM_BYTES),
+    )(jnp.reshape(group * latitudes, (1,)).astype(jnp.int32), legendre)
+
+
 def local(coefficients, rotations, legendre, degree_slot, column_order):
     owners = lax.axis_size("own")
     groups = lax.axis_size("grp")
@@ -180,15 +214,8 @@
     share = slot_count // owners
 
     shared = latitudes % groups == 0
-    mine = legendre
-    if shared:
-        mine = lax.dynamic_slice_in_dim(
-            legendre, lax.axis_index("grp") * (latitudes // groups), latitudes // groups, axis=0
-        )
-    mine = mine.reshape(mine.shape[0], buckets, owners, share, orders)
-    packed = jnp.concatenate([mine[:, b, :, :, slot_count * b :] for b in range(buckets)], axis=-1)
+    packed = pack(legendre, buckets, slot_count, owners, groups if shared else 1)
     lanes = packed.shape[-1]
-    packed = packed.transpose(1, 0, 2, 3).reshape(owners, -1, lanes)
     moved = lax.all_to_all(packed, "own", split_axis=0, concat_axis=0, tiled=True)
 
     degrees = lax.dynamic_slice_in_dim(degree_slot, own_index * slot_local, slot_local, axis=1)
@@ -241,10 +268,8 @@
         (low_arrived, tables_of_blocks[:high])
     )
 
-    def synthesize(blocks, received, after):
+    def synthesize(blocks, received, parts):
         pieces = []
-        if after is not None:
-            received, _ = lax.optimization_barrier((received, after))
         for block in blocks:
             values = jnp.concatenate([received[k][:, block] for k in range(block, buckets)], axis=0)
             summed = jnp.einsum(
@@ -252,20 +277,19 @@
             )
             pieces.append(summed.astype(jnp.bfloat16).reshape(owners, latitudes, share * 2, columns))
         outgoing = jnp.concatenate(pieces, axis=2)
-        return outgoing, lax.all_to_all(outgoing, "own", split_axis=0, concat_axis=0, tiled=True)
+        if parts:
+            outgoing, parts[-1] = lax.optimization_barrier((outgoing, parts[-1]))
+        return lax.all_to_all(outgoing, "own", split_axis=0, concat_axis=0, tiled=True)
 
     longitude = jnp.arange(longitudes, dtype=jnp.int32)
-    low = buckets // 4
     groups_of_blocks = [
         list(range(high, buckets)),
-        list(range(low, high)),
-        list(range(low)),
+        list(range(high)),
     ]
-    parts, tables, after = [], [], None
+    parts, tables = [], []
     received = {**received, **low_arrived}
     for blocks in groups_of_blocks:
-        after, part = synthesize(blocks, received, after if len(parts) == 2 else None)
-        parts.append(part)
+        parts.append(synthesize(blocks, received, parts))
         held = (
             slot_count * jnp.asarray(blocks, jnp.int32)[None, :, None]
             + share * jnp.arange(owners, dtype=jnp.int32)[:, None, None]

time: 533 us -> 521 us (0.977)
  local copies, waits for them, and re-layouts: 115 us -> 89.3 us
  waiting for transfers between devices: 266 us -> 279 us
  Pallas kernels: 63.7 us -> 71.3 us
    all_to_all x3 -> x2, waiting for transfers between devices: 124 us -> 135 us  [synthesize(): lax.all_to_all(outgoing, 'own', split_axis=0, concat_axis=0, tiled=True)]
    transpose x2 -> x0, local copies, waits for them, and re-layouts: 8.39 us -> none  [the longest x1 7.09 us: local(): moved = moved.transpose(1, 0, 2, 3, 4)]
    pallas_call x0 -> x1, Pallas kernels: none -> 6.54 us  [pack(): pl.pallas_call(kernel, grid_spec=pltpu.PrefetchScalarGridSpec(num_scalar_...]
    all_to_all x3 -> x2, starting transfers between devices: 14.9 us -> 10.7 us  [synthesize(): lax.all_to_all(outgoing, 'own', split_axis=0, concat_axis=0, tiled=True)]
    unnamed x88 -> x76, local copies, waits for them, and re-layouts: 46.7 us -> 42.5 us
  transfers between devices with their start and end apart: 7 -> 6, of which waited for: 7 -> 6; matrix products, arithmetic and copies ran while one was open for 23% -> 21% of each run, Pallas kernels for 9% -> 9%
where the time goes in v4:
time: 521 us; the launch traced here: 513 us
  waiting for transfers between devices  279 us (54%)
  local copies, waits for them, and re-layouts  89.3 us (17%)
  Pallas kernels  71.3 us (14%)
  starting transfers between devices  27.7 us (5%)
  other arithmetic  16.6 us (3%)
  matrix products  15.3 us (3%)
  between operations  14.1 us (3%)
    all_to_all x2, waiting for transfers between devices, synthesize(): lax.all_to_all(outgoing, 'own', split_axis=0, concat_axis=0, tiled=True)  135 us
    all_to_all x2, waiting for transfers between devices, local(): lax.all_to_all(outgoing, 'own', split_axis=0, concat_axis=0, tiled=True)  82.7 us
    all_gather x1, waiting for transfers between devices, local(): moved = lax.all_gather(moved, 'grp', axis=0, tiled=False)  54.7 us
    unnamed x76, local copies, waits for them, and re-layouts  42.5 us
    pallas_call x2, Pallas kernels, rotate_classes(): pl.pallas_call(kernel, grid_spec=pltpu.PrefetchScalarGridSpec(num_scalar_...  36.7 us
    pallas_call x1, Pallas kernels, transform(): pl.pallas_call(late, grid=(longitudes // width,), in_specs=[part_spec(par...  19.6 us
    slice x16, local copies, waits for them, and re-layouts, local(): arrived[:, start:start + size]  14.3 us
    all_to_all x2, starting transfers between devices, synthesize(): lax.all_to_all(outgoing, 'own', split_axis=0, concat_axis=0, tiled=True)  10.7 us
  transfers between devices with their start and end apart: 6, of which 6 were waited for; matrix products, arithmetic and copies ran while one was open for 21% of the time, Pallas kernels for 9%

profile of v4, /device:TPU:13, one launch (start us, length us, event | category | flops | bytes accessed | tf_op | source)
XLA Modules:
  0.0 513.5 jit_solution(3633482817918642285)
XLA Ops:
  6.5 6.5 %shard_map.147 = bf16[16,8,4,2304]{3,2,1,0:T(4,128)(2,1)} custom-call(s32[1]{0:T(128)} %bitcast.18._, bf16[16,512,512]{2,1,0:T(8,128)(2,1)} %in_ref.1), custom_call_target="tpu_custom_call" | custom-call | tf_op jit(solution)/shard_map/pallas_call | solution.py:192
  13.1 6.6 %all-to-all-start.1 = ((bf16[16,8,4,2304]{3,2,1,0:T(4,128)(2,1)}), bf16[16,8,4,2304]{3,2,1,0:T(4,128)(2,1)}, u32[]{:S(2)}, u32[]{:S(2)}) async-start(bf16[16,8,4,2304]{3,2,1,0:T(4,128)(2,1)} %shard_map.147), calls=%async_computation.1 | async-start | bytes 4718592 | tf_op jit(solution)/shard_map/all_to_all | solution.py:219
  19.6 8.1 %slice.198 = bf16[4,1048576]{1,0:T(4,128)(2,1)} slice(bf16[4,3342336]{1,0:T(4,128)(2,1)} %param.16), slice={[0:4], [2293760:3342336]} | slice | bytes 16777216 | tf_op jit(solution)/shard_map/slice | solution.py:66
  27.7 9.7 %copy.186 = bf16[1,4,1024,1024]{3,2,1,0:T(8,128)(2,1)} copy(bf16[1,4,1024,1024]{3,1,2,0:T(4,128)(2,1)} %bitcast.263) | data formatting | bytes 16777216
  37.4 3.6 copy.187
  42.3 20.2 %shard_map.145 = (bf16[4,1024,256]{2,1,0:T(8,128)(2,1)}, bf16[4,896,256]{2,1,0:T(8,128)(2,1)}) custom-call(s32[8,4]{1,0:T(8,128)} %dynamic-slice_add_fusion.degree_ref, bf16[4,256,4608]{2,1,0:T(8,128)(2,1)} %coef_ref.3, bf16[256,256]{1,0:T(8,128)(2,1)} %fusion.66.pick_ref, bf16[4,1024,1024]{2,1,0:T(8,128)(2,1)} %bitcast.282, bf16[4,896,896]{2,1,0:T(8,128)(2,1)} %bitcast.288, ...), custom_call_target="tpu_custom_call" | custom-call | flops 7583301632 | bytes 22675456 | tf_op jit(solution)/shard_map/pallas_call | solution.py:71
  62.5 3.6 copy_bitcast_fusion.4
  66.1 6.7 %all-to-all-done.1 = bf16[16,8,4,2304]{3,2,1,0:T(4,128)(2,1)} async-done(((bf16[16,8,4,2304]{3,2,1,0:T(4,128)(2,1)}), bf16[16,8,4,2304]{3,2,1,0:T(4,128)(2,1)}, u32[]{:S(2)}, u32[]{:S(2)}) %all-to-all-start.1) | async-done | bytes 2359328 | tf_op jit(solution)/shard_map/all_to_all | solution.py:219
  72.8 5.3 %all-to-all-start.2 = ((bf16[16,4,120,256]{3,2,1,0:T(8,128)(2,1)}), bf16[16,4,120,256]{3,2,1,0:T(8,128)(2,1)}, u32[]{:S(2)}, u32[]{:S(2)}) async-start(bf16[16,4,120,256]{3,2,1,0:T(8,128)(2,1)} %copy_bitcast_fusion.4), calls=%async_computation.2 | async-start | bytes 7864320 | tf_op jit(solution)/shard_map/all_to_all | solution.py:237
  78.1 2.3 slice-done.1
  80.4 2.8 copy.189
  83.2 2.1 copy.190
  85.3 1.8 copy.191
  90.8 16.5 %shard_map.146 = (bf16[4,768,256]{2,1,0:T(8,128)(2,1)}, bf16[4,640,256]{2,1,0:T(8,128)(2,1)}, bf16[4,512,256]{2,1,0:T(8,128)(2,1)}, bf16[4,384,256]{2,1,0:T(8,12...) custom-call(s32[8,4]{1,0:T(8,128)} %dynamic-slice_add_fusion.degree_ref, ...), custom_call_target="tpu_custom_call" | custom-call | flops 6106906624 | bytes 22937600 | tf_op jit(solution)/shard_map/pallas_call | solution.py:71
  111.3 3.0 copy.188
  114.3 50.4 %all-to-all-done.2 = bf16[16,4,120,256]{3,2,1,0:T(8,128)(2,1)} async-done(((bf16[16,4,120,256]{3,2,1,0:T(8,128)(2,1)}), bf16[16,4,120,256]{3,2,1,0:T(8,128)(2,1)}, u32[]{:S(2)}, u32[]{:S(2)}) %all-to-all-start.2) | async-done | bytes 3932192 | tf_op jit(solution)/shard_map/all_to_all | solution.py:237
  164.7 4.9 all-to-all-start
  169.9 3.4 copy.110
  174.4 1.7 slice.283
  182.1 54.7 %all-gather.3.cloned.1.call-done = bf16[32,8,4,2304]{3,1,2,0:T(8,128)(2,1)} async-done(((bf16[16,8,4,2304]{3,1,2,0:T(8,128)(2,1)}), bf16[32,8,4,2304]{3,1,2,0:T(8,128)(2,1)}) %all-gather.3.cloned.1.call-update) | async-done | bytes 4718608 | tf_op jit(solution)/shard_map/all_gather | solution.py:248
  236.7 4.9 copy.111
  241.7 1.9 convolution_convert_fusion.2
  257.9 32.3 %all-to-all-done = bf16[16,4,168,256]{3,2,1,0:T(8,128)(2,1)} async-done(((bf16[16,4,168,256]{3,2,1,0:T(8,128)(2,1)}), bf16[16,4,168,256]{3,2,1,0:T(8,128)(2,1)}, u32[]{:S(2)}, u32[]{:S(2)}) %all-to-all-start) | async-done | bytes 5505056 | tf_op jit(solution)/shard_map/all_to_all | solution.py:237
  290.2 5.5 %all-to-all-start.3 = ((bf16[16,16,16,256]{3,2,1,0:T(8,128)(2,1)}), bf16[16,16,16,256]{3,2,1,0:T(8,128)(2,1)S(1)}, u32[]{:S(2)}, u32[]{:S(2)}) async-start(bf16[16,16,16,256]{3,2,1,0:T(8,128)(2,1)} %pad_maximum_fusion.1), calls=%async_computation.3 | async-start | bytes 4194304 | tf_op jit(solution)/shard_map/all_to_all | solution.py:282
  321.7 21.3 %all-to-all-done.3.refs_0_ = bf16[16,16,16,256]{3,2,1,0:T(8,128)(2,1)S(1)} async-done(((bf16[16,16,16,256]{3,2,1,0:T(8,128)(2,1)}), bf16[16,16,16,256]{3,2,1,0:T(8,128)(2,1)S(1)}, u32[]{:S(2)}, u32[]{:S(2)}) %all-to-all-start.3) | async-done | bytes 2097184 | tf_op jit(solution)/shard_map/all_to_all | solution.py:282
  344.4 5.2 %all-to-all-start.4 = ((bf16[16,16,48,256]{3,2,1,0:T(8,128)(2,1)}), bf16[16,16,48,256]{3,2,1,0:T(8,128)(2,1)}, u32[]{:S(2)}, u32[]{:S(2)}) async-start(bf16[16,16,48,256]{3,2,1,0:T(8,128)(2,1)} %copy_dynamic-update-slice_fusion), calls=%async_computation.4 | async-start | bytes 12582912 | tf_op jit(solution)/shard_map/all_to_all | solution.py:282
  349.9 2.1 fusion.65
  353.9 6.2 %fusion.37 = (f32[384,1,1024]{2,0,1:T(8,128)S(1)}, f32[384,1,1024]{2,0,1:T(8,128)S(1)}) fusion(s32[384]{0:T(512)S(1)} %add.140), kind=kLoop, calls=%fused_computation.79 | loop fusion | flops 5505024 | bytes 3147264 | tf_op jit(solution)/shard_map/cos | solution.py:300
  362.2 2.3 convert_element_type.177.table_ref
  364.5 8.6 %shard_map.148.sum_ref = f32[16,256,1024]{2,1,0:T(8,128)} custom-call(bf16[16,16,16,256]{3,2,1,0:T(8,128)(2,1)} %copy-done, bf16[256,1024]{1,0:T(8,128)(2,1)} %convert_element_type.180.refs_1_), custom_call_target="tpu_custom_call" | custom-call | flops 2147483648 | bytes 16777216 | tf_op jit(solution)/shard_map/pallas_call | solution.py:147
  373.0 113.8 %all-to-all-done.4.part_ref = bf16[16,16,48,256]{3,2,1,0:T(8,128)(2,1)} async-done(((bf16[16,16,48,256]{3,2,1,0:T(8,128)(2,1)}), bf16[16,16,48,256]{3,2,1,0:T(8,128)(2,1)}, u32[]{:S(2)}, u32[]{:S(2)}) %all-to-all-start.4) | async-done | bytes 6291488 | tf_op jit(solution)/shard_map/all_to_all | solution.py:282
  486.9 19.6 %shard_map.149 = bf16[256,16,1024]{2,1,0:T(8,128)(2,1)} custom-call(bf16[16,16,48,256]{3,2,1,0:T(8,128)(2,1)} %all-to-all-done.4.part_ref, bf16[768,1024]{1,0:T(8,128)(2,1)} %convert_element_type.177.table_ref, f32[16,256,1024]{2,1,0:T(8,128)} %shard_map.148.sum_ref), custom_call_target="tpu_custom_call" | custom-call | tf_op jit(solution)/shard_map/pallas_call | solution.py:160
  (139 shorter events, 62.1 us)
Async XLA Ops:
  13.1 59.7 %all-to-all-start.1 = ((bf16[16,8,4,2304]{3,2,1,0:T(4,128)(2,1)}), bf16[16,8,4,2304]{3,2,1,0:T(4,128)(2,1)}, u32[]{:S(2)}, u32[]{:S(2)}) async-start(bf16[16,8,4,2304]{3,2,1,0:T(4,128)(2,1)} %shard_map.147), calls=%async_computation.1 | async-start | bytes 4718592 | tf_op jit(solution)/shard_map/all_to_all | solution.py:219
  27.7 9.7 %slice-start = ((bf16[4,3342336]{1,0:T(4,128)(2,1)}), bf16[4,802816]{1,0:T(4,128)(2,1)S(1)}, s32[]{:S(2)}) async-start(bf16[4,3342336]{1,0:T(4,128)(2,1)} %param.16), calls=%async_computation.6 | async-start | bytes 12845056 | tf_op jit(solution)/shard_map/slice | solution.py:66
  37.4 3.6 copy-start.22
  37.4 4.2 copy-start.23
  72.8 92.0 %all-to-all-start.2 = ((bf16[16,4,120,256]{3,2,1,0:T(8,128)(2,1)}), bf16[16,4,120,256]{3,2,1,0:T(8,128)(2,1)}, u32[]{:S(2)}, u32[]{:S(2)}) async-start(bf16[16,4,120,256]{3,2,1,0:T(8,128)(2,1)} %copy_bitcast_fusion.4), calls=%async_computation.2 | async-start | bytes 7864320 | tf_op jit(solution)/shard_map/all_to_all | solution.py:237
  78.0 2.3 slice-start.1
  80.4 2.9 slice-start.2
  83.2 2.1 slice-start.3
  85.3 1.8 slice-start.4
  107.4 1.8 copy-start.7
  109.0 1.3 copy-start.8
  109.1 1.3 copy-start.10
  109.2 1.4 copy-start.15
  164.7 125.4 %all-to-all-start = ((bf16[16,4,168,256]{3,2,1,0:T(8,128)(2,1)}), bf16[16,4,168,256]{3,2,1,0:T(8,128)(2,1)}, u32[]{:S(2)}, u32[]{:S(2)}) async-start(bf16[16,4,168,256]{3,2,1,0:T(8,128)(2,1)} %bitcast.270), calls=%async_computation | async-start | bytes 11010048 | tf_op jit(solution)/shard_map/all_to_all | solution.py:237
  169.6 67.1 %all-gather.3.cloned.1.call-start = ((), (), s32[]{:S(2)}) async-start(), calls=%async_computation.5 | async-start | bytes 7077888 | tf_op jit(solution)/shard_map/all_gather | solution.py:248
  179.0 66.1 %copy-start.2 = (bf16[64,64,256]{2,0,1:T(8,128)(2,1)}, bf16[64,64,256]{2,0,1:T(8,128)(2,1)S(1)}, u32[]{:S(2)}) copy-start(bf16[64,64,256]{2,0,1:T(8,128)(2,1)S(1)} %copy.116) | copy-start | bytes 6291460
  179.4 1.5 copy-start.4
  243.5 1.6 copy-start.13
  246.8 1.2 copy-start.6
  246.8 3.3 copy-start.1
  290.2 52.8 %all-to-all-start.3 = ((bf16[16,16,16,256]{3,2,1,0:T(8,128)(2,1)}), bf16[16,16,16,256]{3,2,1,0:T(8,128)(2,1)S(1)}, u32[]{:S(2)}, u32[]{:S(2)}) async-start(bf16[16,16,16,256]{3,2,1,0:T(8,128)(2,1)} %pad_maximum_fusion.1), calls=%async_computation.3 | async-start | bytes 4194304 | tf_op jit(solution)/shard_map/all_to_all | solution.py:282
  305.3 1.5 copy-start.5
  305.4 2.1 copy-start.3
  306.9 1.2 copy-start.19
  306.9 1.3 copy-start.20
  307.5 1.2 copy-start.18
  310.0 1.6 copy-start.9
  311.6 2.3 copy-start.11
  313.9 2.3 copy-start.12
  321.7 27.9 %copy-start.24 = (s32[2]{0:T(128)S(1)}, s32[2]{0:T(128)}, u32[]{:S(2)}) copy-start(s32[2]{0:T(128)} %constant.82) | copy-start | bytes 28
  343.0 1.4 copy-start
  344.4 142.5 %all-to-all-start.4 = ((bf16[16,16,48,256]{3,2,1,0:T(8,128)(2,1)}), bf16[16,16,48,256]{3,2,1,0:T(8,128)(2,1)}, u32[]{:S(2)}, u32[]{:S(2)}) async-start(bf16[16,16,48,256]{3,2,1,0:T(8,128)(2,1)} %copy_dynamic-update-slice_fusion), calls=%async_computation.4 | async-start | bytes 12582912 | tf_op jit(solution)/shard_map/all_to_all | solution.py:282
  (5 other events, 5.7 us)
Sparse Core Ops, SparseCore 0:
  173.5 63.2 all-gather.2
